TPU v7x, 256 devices: a whole 4x4x8 slice. The times are simulated.
256 devices in a mesh: member: 32 (over y, z), tile: 8 (over x, core).
Axes of the slice: x: 4, y: 4, z: 8, core: 2. Of those that a mesh axis runs over, the one named last changes fastest.
Arguments:
- realization_array: float32 [32, 4, 512, 512], P('member', None, 'tile'), may hold values from -6 to 6
- water_depth: float32 [512, 512], P('tile'), may hold values from 0.5 to 4
- wet_mask: int32 [512, 512], P('tile'), may hold values 0 or 1
- obs_cell: int32 [32768], P('tile'), may hold values from 0 to 32767, as said below
- obs_value: float32 [32768], P('tile'), may hold values from -8 to 8
- obs_error: float32 [32768], P('tile'), may hold values from 0.05 to 0.5
- celer_gain: float32 [32768], P('tile'), may hold values from 0.5 to 2
- obs_list: int32 [8, 128, 64], P('tile', 'member'), may hold values from 3584 to 8639, as said below
- obs_count: int32 [8, 128], P('tile', 'member'), may hold values from 32 to 64, as said below
Outputs:
- analysis: float32 [32, 4, 512, 512], P('member', None, 'tile')
Inputs may be any that keep to these rules, and one draw needn't show every extreme that they name: `obs_cell`: observation o of a tile lies in cells o * S to o * S + S - 1 of that tile, S = 8. `obs_list`: the entries of one patch's list are distinct and name only observations of existing tiles. `obs_count`: some patch has a full list.
All inputs are finite; a program needn't handle non-finite values. No bound on the sum of `wet_mask` on one device may be relied on, other than what follows from the above.
Results may differ from a plain program's by a relative error of at most 0.0003.
Values sent between devices are 32-bit elements; how exact they have to be, the bound alone decides.
A program may use at most 128 MiB of HBM per device.

v0:
```python
import jax
import jax.numpy as jnp
from jax import lax
from jax.sharding import PartitionSpec as P

REGION_POINTS = 256
STEPS = 4
NS_ITERS = 14


FRICTION = 0.98
PRESSURE = 0.25
DIVERGE = 0.25
FORCING = 0.05
UPWIND = 0.4
DAMPING = 0.02
HIGH = lax.Precision.HIGHEST


def padded_2(block, sides, width):
    for axis, dim in sides:
        count = lax.axis_size(axis)
        forward = [(i, i + 1) for i in range(count - 1)]
        backward = [(target, source) for source, target in forward]
        low = lax.ppermute(
            lax.slice_in_dim(block, block.shape[dim] - width, None, axis=dim), axis, forward
        )
        high = lax.ppermute(lax.slice_in_dim(block, 0, width, axis=dim), axis, backward)
        block = jnp.concatenate([low, block, high], axis=dim)
    return block


def along_y(field):
    padded = jnp.pad(field, ((0, 0), (1, 1)))
    return (padded[:, 2:], padded[:, :-2])


def mat_mul(left, right):
    return jnp.matmul(left, right, precision=HIGH)


def mix_weights(gram, proj):
    count = gram.shape[-1]
    eye = jnp.eye(count, dtype=jnp.float32)
    amat = gram + (count - 1.0) * eye
    trace_sum = jnp.trace(amat, axis1=1, axis2=2)
    current = amat / trace_sum[:, None, None]
    inverse = jnp.broadcast_to(eye, amat.shape)
    for sweep in range(NS_ITERS):
        factor = 1.5 * eye - 0.5 * mat_mul(inverse, current)
        current = mat_mul(current, factor)
        inverse = mat_mul(factor, inverse)
    root = inverse / jnp.sqrt(trace_sum)[:, None, None]
    covar = mat_mul(root, root)
    wbar = jnp.einsum("pkl,pl->pk", covar, proj, precision=HIGH)
    wtot = jnp.sqrt(count - 1.0) * root + wbar[:, :, None]
    return wtot - jnp.mean(wtot, axis=1, keepdims=True) + 1.0 / count


def body(
    realization_array,
    water_depth,
    wet_mask,
    obs_cell,
    obs_value,
    obs_error,
    celer_gain,
    obs_list,
    obs_count,
):
    wet_float = wet_mask.astype(jnp.float32)
    grid_rows, cell_width = water_depth.shape
    state = realization_array[0]
    water_elevation, eastward_velocity, northward_velocity, swell_intensity = (
        state[0],
        state[1],
        state[2],
        state[3],
    )
    for sweep in range(STEPS):
        extended = padded_2(jnp.stack([water_elevation, swell_intensity]), (("tile", 1),), 1)
        level_ext = extended[0]
        energy_ext = extended[1]
        new_x = wet_float * (
            FRICTION * eastward_velocity - PRESSURE * (level_ext[2:] - level_ext[:-2])
        )
        level_up, level_down = along_y(water_elevation)
        new_y = wet_float * (FRICTION * northward_velocity - PRESSURE * (level_up - level_down))
        flux_x = padded_2(water_depth * new_x, (("tile", 0),), 1)
        flux_up, flux_down = along_y(water_depth * new_y)
        new_surface = wet_float * (
            water_elevation
            - DIVERGE * (flux_x[2:] - flux_x[:-2] + flux_up - flux_down)
            + FORCING * swell_intensity
        )
        new_energy = wet_float * (
            swell_intensity
            - UPWIND * (swell_intensity - energy_ext[:-2])
            - DAMPING * swell_intensity
        )
        water_elevation, eastward_velocity, northward_velocity, swell_intensity = (
            new_surface,
            new_x,
            new_y,
            new_energy,
        )
    obs_tile = obs_cell.shape[0]
    radius = obs_tile // 8
    equiv = celer_gain * water_elevation.reshape(-1)[obs_cell]
    all_equiv = lax.all_gather(equiv[None], "member", axis=0, tiled=True)
    stacked = jnp.concatenate([all_equiv, obs_value[None], obs_error[None]], axis=0)
    stack_ext = padded_2(stacked, (("tile", 1),), radius)
    win_equiv = stack_ext[:-2]
    win_value = stack_ext[-2]
    win_error = stack_ext[-1]
    realization_pile = win_equiv.shape[0]
    indices = obs_list[0]
    counts = obs_count[0]
    per_dev = indices.shape[0]
    patch_index = lax.axis_index("member") * per_dev + jnp.arange(per_dev, dtype=jnp.int32)
    row_index = patch_index * REGION_POINTS // cell_width
    centre = obs_tile + row_index * obs_tile // grid_rows
    positions = indices - (obs_tile - radius)
    picked = win_equiv[:, positions]
    value = win_value[positions]
    error = win_error[positions]
    dist = (indices - centre[:, None]).astype(jnp.float32) / radius
    live = jnp.arange(indices.shape[1], dtype=jnp.int32)[None, :] < counts[:, None]
    precision = jnp.where(live, 1.0 / ((1.0 + 4.0 * dist * dist) * error), 0.0)
    mean_eq = jnp.mean(picked, axis=0)
    spread = jnp.transpose(picked - mean_eq[None], (1, 0, 2))
    weighted = spread * precision[:, None, :]
    gram = jnp.matmul(weighted, jnp.swapaxes(spread, 1, 2), precision=HIGH)
    innovation = (precision * (value - mean_eq))[:, :, None]
    proj = jnp.matmul(spread, innovation, precision=HIGH)[:, :, 0]
    mix = mix_weights(gram, proj)
    predicted_fields = jnp.stack(
        [water_elevation, eastward_velocity, northward_velocity, swell_intensity]
    ).reshape(1, 4, grid_rows * cell_width)
    region_fields = lax.all_to_all(
        predicted_fields, "member", split_axis=2, concat_axis=0, tiled=True
    )
    fields = region_fields.shape[1]
    panel_sequence = region_fields.reshape(realization_pile, fields, per_dev, REGION_POINTS)
    mixed = jnp.einsum("kfpc,pkm->mfpc", panel_sequence, mix, precision=HIGH)
    result = lax.all_to_all(
        mixed.reshape(realization_pile, fields, per_dev * REGION_POINTS),
        "member",
        split_axis=0,
        concat_axis=2,
        tiled=True,
    )
    return result.reshape(1, 4, grid_rows, cell_width)


def solution(mesh):
    return jax.shard_map(
        body,
        mesh=mesh,
        in_specs=(
            P("member", None, "tile", None),
            P("tile", None),
            P("tile", None),
            P("tile"),
            P("tile"),
            P("tile"),
            P("tile"),
            P("tile", "member", None),
            P("tile", "member"),
        ),
        out_specs=P("member", None, "tile", None),
        check_vma=False,
    )
```

profile of v0, /device:TPU:5, one launch (start us, length us, event | category | flops | bytes accessed | tf_op | source)
XLA Modules:
  0.0 423.1 jit_solution(1475901937821299009)
XLA Ops:
  1.1 2.6 collective-permute-start
  3.7 3.0 collective-permute-start.1
  7.4 1.3 fusion.136
  8.7 3.1 collective-permute-start.2
  11.8 3.0 collective-permute-start.3
  16.7 3.1 collective-permute-start.4
  19.9 3.0 collective-permute-start.5
  23.6 1.2 fusion.132
  24.8 3.1 collective-permute-start.6
  28.0 3.0 collective-permute-start.7
  32.7 3.1 collective-permute-start.8
  35.9 3.0 collective-permute-start.9
  40.7 3.1 collective-permute-start.10
  43.9 3.0 collective-permute-start.11
  48.6 3.1 collective-permute-start.12
  51.8 3.0 collective-permute-start.13
  56.7 3.1 collective-permute-start.14
  59.8 3.0 collective-permute-start.15
  64.8 23.0 %gather_fusion = f32[4096]{0:T(1024)S(1)} fusion(f32[32768]{0:T(1024)S(1)} %bitcast.270, s32[4096]{0:T(1024)S(1)} %fusion.115), kind=kCustom, calls=%fused_computation | custom fusion | bytes 49152 | tf_op jit(solution)/shard_map/gather | solution.py:109
  87.8 41.0 %all-gather = f32[131072]{0:T(1024)S(1)} all-gather(f32[4096]{0:T(1024)S(1)} %mul.405), channel_id=2, replica_groups=mesh['member'=32,'tile'=8] {'member'}, dimensions={0}, use_global_device_ids=true | all-gather | bytes 540672 | tf_op jit(solution)/shard_map/all_gather | solution.py:110
  129.0 15.9 %collective-permute-start.16 = (f32[34,512]{1,0:T(8,128)S(1)}, f32[34,512]{1,0:T(8,128)S(1)}, u32[]{:S(2)}, u32[]{:S(2)}) collective-permute-start(f32[34,512]{1,0:T(8,128)S(1)} %get-tuple-element.23), channel_id=1, source_target_pairs={{0,1},{1,2},{2,3},{3,4},{4,5},{5,6},{6,7},{8,9},{9,10},{10,11},{11... | collective-permute-start | bytes 208904 | tf_op jit(solution)/shard_map/ppermute | solution.py:25
  144.9 1.9 collective-permute-start.17
  147.4 23.9 %copy.28 = f32[1,4,32768]{1,0,2:T(1,128)} copy(f32[1,4,32768]{2,1,0:T(4,128)S(1)} %pad_maximum_fusion.1) | data formatting | bytes 1048576 | tf_op jit(solution)/shard_map/stack | solution.py:137
  171.8 146.5 %reduce.1 = f32[32768,4]{1,0:T(8,128)} reduce(f32[32768,1,4]{2,1,0:T(1,128)} %bitcast.273, f32[]{:T(128)} %broadcast.390), dimensions={1}, to_apply=%bitcast.170.reduce_sub_computation | reduce | bytes 1048580
  318.4 16.0 %reshape.276 = f32[32,1,4096]{2,1,0:T(1,128)} reshape(f32[32768,4]{1,0:T(8,128)} %reduce.1) | data formatting | bytes 1048576
  334.4 6.2 %all-to-all-start = ((f32[32,1,4096]{2,1,0:T(1,128)}), f32[32,1,4096]{2,1,0:T(1,128)}, u32[]{:S(2)}, u32[]{:S(2)}) async-start(f32[32,1,4096]{2,1,0:T(1,128)} %reshape.276), calls=%async_computation | async-start | bytes 1048576 | tf_op jit(solution)/shard_map/all_to_all | solution.py:140
  340.6 1.7 gather_fusion.2
  342.4 1.7 gather_fusion.3
  355.5 2.9 reduce.2
  358.5 29.2 %reshape.277 = f32[32768,1,4]{2,1,0:T(1,128)} reshape(f32[32,4096]{1,0:T(8,128)S(1)} %reduce.2) | data formatting | bytes 1048576
  387.6 10.0 %copy.29 = f32[1,4,32,1024]{3,2,1,0:T(8,128)S(1)} copy(f32[1,4,32,1024]{1,3,2,0:T(8,128)} %bitcast.274) | data formatting | bytes 1048576 | tf_op jit(solution)/shard_map/all_to_all | solution.py:140
  399.4 22.5 %all_to_all.30 = f32[32,4,1024]{2,1,0:T(4,128)S(1)} all-to-all(f32[32,4,1024]{2,1,0:T(4,128)S(1)} %reshape.275), channel_id=1, replica_groups=mesh['member'=32,'tile'=8] {'member'}, dimensions={0} | all-to-all | bytes 1048576 | tf_op jit(solution)/shard_map/all_to_all | solution.py:146
  (127 shorter events, 28.7 us)
Async XLA Ops:
  0.0 87.8 %copy-start.2 = (f32[4096]{0:T(1024)S(1)}, f32[4096]{0:T(1024)}, u32[]{:S(2)}) copy-start(f32[4096]{0:T(1024)} %param.15) | copy-start | bytes 49156
  0.0 128.9 %copy-start = (f32[4096]{0:T(1024)S(1)}, f32[4096]{0:T(1024)}, u32[]{:S(2)}) copy-start(f32[4096]{0:T(1024)} %param.14) | copy-start | bytes 49156
  0.0 129.0 %copy-start.1 = (f32[4096]{0:T(1024)S(1)}, f32[4096]{0:T(1024)}, u32[]{:S(2)}) copy-start(f32[4096]{0:T(1024)} %param.13) | copy-start | bytes 49156
  1.1 6.3 %collective-permute-start = (f32[2,1,512]{2,1,0:T(1,128)S(1)}, f32[2,1,512]{2,1,0:T(1,128)S(1)}, u32[]{:S(2)}, u32[]{:S(2)}) collective-permute-start(f32[2,1,512]{2,1,0:T(1,128)S(1)} %get-tuple-element.42), channel_id=1, source_target_pairs={{1,0},{2,1},{3,2},{4,3},{5,4},{6,5},{7,6},{9,8},{10,9},{11,10},{12... | collective-permute-start | bytes 12296 | tf_op jit(solution)/shard_map/ppermute | solution.py:28
  3.7 3.7 collective-permute-start.1
  8.7 6.8 %collective-permute-start.2 = (f32[1,512]{1,0:T(1,128)S(1)}, f32[1,512]{1,0:T(1,128)S(1)}, u32[]{:S(2)}, u32[]{:S(2)}) collective-permute-start(f32[1,512]{1,0:T(1,128)S(1)} %get-tuple-element.50), channel_id=1, source_target_pairs={{1,0},{2,1},{3,2},{4,3},{5,4},{6,5},{7,6},{9,8},{10,9},{11,10},{12... | collective-permute-start | bytes 6152 | tf_op jit(solution)/shard_map/ppermute | solution.py:28
  11.8 3.7 collective-permute-start.3
  16.7 6.1 %collective-permute-start.4 = (f32[2,1,512]{2,1,0:T(1,128)S(1)}, f32[2,1,512]{2,1,0:T(1,128)S(1)}, u32[]{:S(2)}, u32[]{:S(2)}) collective-permute-start(f32[2,1,512]{2,1,0:T(1,128)S(1)} %get-tuple-element.40), channel_id=1, source_target_pairs={{1,0},{2,1},{3,2},{4,3},{5,4},{6,5},{7,6},{9,8},{10,9},{11,10},{12... | collective-permute-start | bytes 12296 | tf_op jit(solution)/shard_map/ppermute | solution.py:28
  19.9 3.7 collective-permute-start.5
  24.8 6.1 %collective-permute-start.6 = (f32[1,512]{1,0:T(1,128)S(1)}, f32[1,512]{1,0:T(1,128)S(1)}, u32[]{:S(2)}, u32[]{:S(2)}) collective-permute-start(f32[1,512]{1,0:T(1,128)S(1)} %get-tuple-element.48), channel_id=1, source_target_pairs={{1,0},{2,1},{3,2},{4,3},{5,4},{6,5},{7,6},{9,8},{10,9},{11,10},{12... | collective-permute-start | bytes 6152 | tf_op jit(solution)/shard_map/ppermute | solution.py:28
  28.0 3.7 collective-permute-start.7
  32.7 6.1 %collective-permute-start.8 = (f32[2,1,512]{2,1,0:T(1,128)S(1)}, f32[2,1,512]{2,1,0:T(1,128)S(1)}, u32[]{:S(2)}, u32[]{:S(2)}) collective-permute-start(f32[2,1,512]{2,1,0:T(1,128)S(1)} %get-tuple-element.36), channel_id=1, source_target_pairs={{1,0},{2,1},{3,2},{4,3},{5,4},{6,5},{7,6},{9,8},{10,9},{11,10},{12... | collective-permute-start | bytes 12296 | tf_op jit(solution)/shard_map/ppermute | solution.py:28
  35.9 3.7 collective-permute-start.9
  40.7 6.2 %collective-permute-start.10 = (f32[1,512]{1,0:T(1,128)S(1)}, f32[1,512]{1,0:T(1,128)S(1)}, u32[]{:S(2)}, u32[]{:S(2)}) collective-permute-start(f32[1,512]{1,0:T(1,128)S(1)} %get-tuple-element.46), channel_id=1, source_target_pairs={{1,0},{2,1},{3,2},{4,3},{5,4},{6,5},{7,6},{9,8},{10,9},{11,10},{12... | collective-permute-start | bytes 6152 | tf_op jit(solution)/shard_map/ppermute | solution.py:28
  43.9 3.7 collective-permute-start.11
  48.6 6.1 %collective-permute-start.12 = (f32[2,1,512]{2,1,0:T(1,128)S(1)}, f32[2,1,512]{2,1,0:T(1,128)S(1)}, u32[]{:S(2)}, u32[]{:S(2)}) collective-permute-start(f32[2,1,512]{2,1,0:T(1,128)S(1)} %get-tuple-element.33), channel_id=1, source_target_pairs={{1,0},{2,1},{3,2},{4,3},{5,4},{6,5},{7,6},{9,8},{10,9},{11,10},{12... | collective-permute-start | bytes 12296 | tf_op jit(solution)/shard_map/ppermute | solution.py:28
  51.8 3.7 collective-permute-start.13
  56.7 6.6 %collective-permute-start.14 = (f32[1,512]{1,0:T(1,128)S(1)}, f32[1,512]{1,0:T(1,128)S(1)}, u32[]{:S(2)}, u32[]{:S(2)}) collective-permute-start(f32[1,512]{1,0:T(1,128)S(1)} %get-tuple-element.44), channel_id=1, source_target_pairs={{1,0},{2,1},{3,2},{4,3},{5,4},{6,5},{7,6},{9,8},{10,9},{11,10},{12... | collective-permute-start | bytes 6152 | tf_op jit(solution)/shard_map/ppermute | solution.py:28
  59.8 3.7 collective-permute-start.15
  129.0 211.6 %collective-permute-start.16 = (f32[34,512]{1,0:T(8,128)S(1)}, f32[34,512]{1,0:T(8,128)S(1)}, u32[]{:S(2)}, u32[]{:S(2)}) collective-permute-start(f32[34,512]{1,0:T(8,128)S(1)} %get-tuple-element.23), channel_id=1, source_target_pairs={{0,1},{1,2},{2,3},{3,4},{4,5},{5,6},{6,7},{8,9},{9,10},{10,11},{11... | collective-permute-start | bytes 208904 | tf_op jit(solution)/shard_map/ppermute | solution.py:25
  144.9 195.6 %collective-permute-start.17 = (f32[34,512]{1,0:T(8,128)S(1)}, f32[34,512]{1,0:T(8,128)S(1)}, u32[]{:S(2)}, u32[]{:S(2)}) collective-permute-start(f32[34,512]{1,0:T(8,128)S(1)} %get-tuple-element.24), channel_id=1, source_target_pairs={{1,0},{2,1},{3,2},{4,3},{5,4},{6,5},{7,6},{9,8},{10,9},{11,10},{12... | collective-permute-start | bytes 208904 | tf_op jit(solution)/shard_map/ppermute | solution.py:28
  318.4 27.8 %copy-start.3 = (s32[1,4,64]{2,1,0:T(4,128)S(1)}, s32[1,4,64]{2,1,0:T(4,128)}, u32[]{:S(2)}) copy-start(s32[1,4,64]{2,1,0:T(4,128)} %param.16) | copy-start | bytes 3076
  318.4 27.8 %copy-start.4 = (s32[1,4]{1,0:T(1,128)S(1)}, s32[1,4]{1,0:T(1,128)}, u32[]{:S(2)}) copy-start(s32[1,4]{1,0:T(1,128)} %param.17) | copy-start | bytes 52
  334.4 21.2 %all-to-all-start = ((f32[32,1,4096]{2,1,0:T(1,128)}), f32[32,1,4096]{2,1,0:T(1,128)}, u32[]{:S(2)}, u32[]{:S(2)}) async-start(f32[32,1,4096]{2,1,0:T(1,128)} %reshape.276), calls=%async_computation | async-start | bytes 1048576 | tf_op jit(solution)/shard_map/all_to_all | solution.py:140
where the time goes:
time: 428 us; the launch traced here: 423 us
  other arithmetic  161 us (38%)
  local copies, waits for them, and re-layouts  112 us (26%)
  starting transfers between devices  72.3 us (17%)
  blocking collectives  63.5 us (15%)
  matrix products  9.54 us (2%)
    unnamed x1, other arithmetic  147 us
    unnamed x15, local copies, waits for them, and re-layouts  46.7 us
    all_gather x1, blocking collectives, body(): all_equiv = lax.all_gather(equiv[None], 'member', axis=0, tiled=True)  41 us
    ppermute x9, starting transfers between devices, padded_2(): lax.ppermute(lax.slice_in_dim(block, block.shape[dim] - width, None, axis...  39.8 us
    ppermute x9, starting transfers between devices, padded_2(): lax.ppermute(lax.slice_in_dim(block, 0, width, axis=dim), axis, backward)  26.4 us
    another operation x5, local copies, waits for them, and re-layouts, body(): jnp.stack([water_elevation, eastward_velocity, northward_velocity, swell_...  24.5 us
    gather x1, local copies, waits for them, and re-layouts, body(): equiv = celer_gain * water_elevation.reshape(-1)[obs_cell]  23 us
    all_to_all x1, blocking collectives, body(): lax.all_to_all(mixed.reshape(realization_pile, fields, per_dev * REGION_P...  22.5 us
  transfers between devices with their start and end apart: 19, of which 6 were waited for; matrix products, arithmetic and copies ran while one was open for 48% of the time, Pallas kernels for 0%

commit v1 on v0

v1 whole, which is shorter than its diff:
```python
import functools

import jax
import jax.numpy as jnp
from jax import lax
from jax.experimental import pallas as pl
from jax.experimental.pallas import tpu as pltpu
from jax.sharding import PartitionSpec as P

MESH = pl.DeviceIdType.MESH
HIGH = lax.Precision.HIGHEST
F32 = jnp.float32
BF16 = jnp.bfloat16

REGION_POINTS = 256
STEPS = 4
NS_ITERS = 14
SPACING = 8

FRICTION = 0.98
PRESSURE = 0.25
DIVERGE = 0.25
FORCING = 0.05
UPWIND = 0.4
DAMPING = 0.02

LANES = 128
GUARD = 8
HALO = 16
OBS_HALO = 8
TABLE_PAD = 8


def iota(shape, dim):
    return lax.broadcasted_iota(jnp.int32, shape, dim)


def dot(left, right, precision=None):
    return lax.dot_general(
        left, right, (((1,), (0,)), ((), ())), precision=precision, preferred_element_type=F32
    )


def split(x):
    high = x.astype(BF16)
    return high, (x - high.astype(F32)).astype(BF16)


def dot3(left, right):
    left_high, left_low = split(left)
    right_high, right_low = split(right)
    return (dot(left_low, right_high) + dot(left_high, right_low)) + dot(left_high, right_high)


def lookup(table, first, last, high, low):
    found = jnp.zeros(high.shape, table.dtype)
    for row in range(first, last):
        line = jnp.broadcast_to(table[row : row + 1, :], high.shape)
        found = jnp.where(
            high == row,
            jnp.take_along_axis(line, low, axis=1, mode="promise_in_bounds"),
            found,
        )
    return found


def kernel(
    members,
    tiles,
    grid_rows,
    state_ref,
    depth_ref,
    wet_ref,
    cell_ref,
    gain_ref,
    value_ref,
    error_ref,
    list_ref,
    count_ref,
    out_ref,
    state_ext,
    depth_ext,
    wet_ext,
    cell_ext,
    gain_ext,
    value_ext,
    error_ext,
    work,
    hwork,
    wwork,
    flux,
    cross,
    pack,
    lists,
    table,
    pick_out,
    pick_in,
    slab_out,
    slab_in,
    mix_out,
    back_in,
    rows_out,
    local_sem,
    halo_send,
    halo_recv,
    group_send,
    group_recv,
):
    me = lax.axis_index("member")
    tile = lax.axis_index("tile")
    above = lax.rem(tile + tiles - 1, tiles)
    below = lax.rem(tile + 1, tiles)
    ext_rows = grid_rows + 2 * HALO
    lane_tiles = 4
    obs_tile = grid_rows * 64
    radius = obs_tile // 8
    own_table = obs_tile // LANES
    table_rows = own_table + 2 * TABLE_PAD
    others = members - 1

    own_rows = pl.ds(HALO, grid_rows)
    own_lines = pl.ds(TABLE_PAD, own_table)
    tables = (
        (cell_ref, cell_ext),
        (gain_ref, gain_ext),
        (value_ref, value_ext),
        (error_ref, error_ext),
    )
    local = [
        pltpu.make_async_copy(state_ref.at[0], state_ext.at[:, own_rows], local_sem.at[0]),
        pltpu.make_async_copy(depth_ref, depth_ext.at[own_rows], local_sem.at[1]),
        pltpu.make_async_copy(wet_ref, wet_ext.at[own_rows], local_sem.at[2]),
    ] + [
        pltpu.make_async_copy(ref, ext.at[own_lines], local_sem.at[3 + i])
        for i, (ref, ext) in enumerate(tables)
    ]
    for copy in local:
        copy.start()

    pack[...] = jnp.zeros(pack.shape, jnp.int32)
    pack[0:4, 0:64] = list_ref[0]
    packed = pack[...]
    turned = pltpu.roll(packed, 64, axis=1)
    left_half = iota((1, LANES), 1) < 64
    own_list = jnp.concatenate(
        [
            jnp.where(left_half, packed[0:1], turned[1:2]),
            jnp.where(left_half, packed[2:3], turned[3:4]),
        ],
        axis=0,
    )
    lists[me] = own_list

    barrier = pltpu.get_barrier_semaphore()

    def greet(step, carry):
        peer = lax.rem(me + step, members)
        pl.semaphore_signal(barrier, inc=1, device_id={"member": peer}, device_id_type=MESH)
        return carry

    pl.semaphore_signal(barrier, inc=1, device_id={"tile": above}, device_id_type=MESH)
    pl.semaphore_signal(barrier, inc=1, device_id={"tile": below}, device_id_type=MESH)
    lax.fori_loop(1, members, greet, 0)
    pl.semaphore_wait(barrier, others + 2)

    halos = []
    for way, (target, source_row, target_row, source_line, target_line) in enumerate(
        (
            (below, grid_rows - HALO, 0, own_table - TABLE_PAD, 0),
            (above, 0, HALO + grid_rows, 0, TABLE_PAD + own_table),
        )
    ):
        source_rows, target_rows = pl.ds(source_row, HALO), pl.ds(target_row, HALO)
        source_lines, target_lines = pl.ds(source_line, TABLE_PAD), pl.ds(target_line, TABLE_PAD)
        pairs = [
            (state_ref.at[0, :, source_rows], state_ext.at[:, target_rows]),
            (depth_ref.at[source_rows], depth_ext.at[target_rows]),
            (wet_ref.at[source_rows], wet_ext.at[target_rows]),
        ] + [(ref.at[source_lines], ext.at[target_lines]) for ref, ext in tables]
        for i, (source, destination) in enumerate(pairs):
            copy = pltpu.make_async_remote_copy(
                src_ref=source,
                dst_ref=destination,
                send_sem=halo_send.at[way, i],
                recv_sem=halo_recv.at[way, i],
                device_id={"tile": target},
                device_id_type=MESH,
            )
            copy.start()
            halos.append(copy)

    def to_group(which, source, destination):
        def send(step, carry):
            peer = lax.rem(me + step, members)
            pltpu.make_async_remote_copy(
                src_ref=source(peer),
                dst_ref=destination,
                send_sem=group_send.at[which],
                recv_sem=group_recv.at[which],
                device_id={"member": peer},
                device_id_type=MESH,
            ).start()
            return carry

        lax.fori_loop(1, members, send, 0)

    def group_done(sems, which, ref, size):
        part = ref.at[pl.ds(0, size)]
        pltpu.make_async_copy(part, part, sems.at[which]).wait()

    to_group(0, lambda peer: lists.at[me], lists.at[me])

    blank = jnp.zeros((lane_tiles, GUARD, LANES), F32)
    for field in range(4):
        work[field, :, 0:GUARD, :] = blank
        work[field, :, GUARD + ext_rows :, :] = blank
    flux[:, 0:GUARD, :] = blank
    flux[:, GUARD + ext_rows :, :] = blank

    for copy in local:
        copy.wait()
    for copy in halos:
        copy.wait_recv()

    for start in range(0, ext_rows, 8):
        rows = slice(start, start + 8)
        put = slice(GUARD + start, GUARD + start + 8)
        if start < HALO:
            inside = tile > 0
        elif start >= HALO + grid_rows:
            inside = tile < tiles - 1
        else:
            inside = None
        for at in range(lane_tiles):
            lanes = slice(at * LANES, (at + 1) * LANES)
            parts = [state_ext[field, rows, lanes] for field in range(4)]
            parts.append(wet_ext[rows, lanes].astype(F32))
            if inside is not None:
                parts = [jnp.where(inside, part, 0.0) for part in parts]
            for field in range(4):
                work[field, at, put, :] = parts[field]
            wwork[at, put, :] = parts[4]
            hwork[at, put, :] = depth_ext[rows, lanes]

    first_lane = iota((8, LANES), 1) == 0
    last_lane = iota((8, LANES), 1) == LANES - 1

    def across(parts):
        nothing = jnp.zeros((8, LANES), F32)
        up = [pltpu.roll(part, LANES - 1, axis=1) for part in parts] + [nothing]
        down = [nothing] + [pltpu.roll(part, 1, axis=1) for part in parts]
        return [
            jnp.where(last_lane, up[at + 1], up[at])
            - jnp.where(first_lane, down[at], down[at + 1])
            for at in range(lane_tiles)
        ]

    def advance(step, carry):
        for start in range(GUARD, GUARD + ext_rows, 8):
            rows = slice(start, start + 8)
            after = slice(start + 1, start + 9)
            before = slice(start - 1, start + 7)
            slope_y = across([work[0, at, rows, :] for at in range(lane_tiles)])
            flow = []
            for at in range(lane_tiles):
                wet = wwork[at, rows, :]
                height = hwork[at, rows, :]
                slope_x = work[0, at, after, :] - work[0, at, before, :]
                new_x = wet * (FRICTION * work[1, at, rows, :] - PRESSURE * slope_x)
                new_y = wet * (FRICTION * work[2, at, rows, :] - PRESSURE * slope_y[at])
                work[1, at, rows, :] = new_x
                work[2, at, rows, :] = new_y
                flux[at, rows, :] = height * new_x
                flow.append(height * new_y)
            for at, part in enumerate(across(flow)):
                cross[at, rows, :] = part
        for start in range(GUARD + ext_rows - 8, 0, -8):
            rows = slice(start, start + 8)
            after = slice(start + 1, start + 9)
            before = slice(start - 1, start + 7)
            for at in range(lane_tiles):
                wet = wwork[at, rows, :]
                level = work[0, at, rows, :]
                energy = work[3, at, rows, :]
                spill = (flux[at, after, :] - flux[at, before, :]) + cross[at, rows, :]
                work[0, at, rows, :] = wet * (level - DIVERGE * spill + FORCING * energy)
                work[3, at, rows, :] = wet * (
                    energy - UPWIND * (energy - work[3, at, before, :]) - DAMPING * energy
                )
        return carry

    lax.fori_loop(0, STEPS, advance, 0)

    first_line = TABLE_PAD - OBS_HALO // 2
    last_line = TABLE_PAD + own_table + OBS_HALO // 2
    offset = (cell_ext[...] & (SPACING - 1)).astype(BF16)
    place = iota((1, LANES), 1) & (SPACING - 1)
    equiv = jnp.zeros((table_rows, LANES), F32)
    for parity in range(2):
        for at in range(lane_tiles):
            owner = iota((LANES, LANES), 0) // SPACING + (parity * 64 + at * 16)
            gather = (owner == iota((LANES, LANES), 1)).astype(BF16)
            owner_t = iota((LANES, LANES), 1) // SPACING + (parity * 64 + at * 16)
            scatter = (owner_t == iota((LANES, LANES), 0)).astype(BF16)
            wanted = dot(offset, scatter).astype(jnp.int32) == place
            level = work[0, at, pl.ds(GUARD + parity, table_rows, stride=2), :]
            level = jnp.where(wanted, level, 0.0)
            high, rest = split(level)
            middle, low = split(level - high.astype(F32))
            equiv = equiv + ((dot(low, gather) + dot(middle, gather)) + dot(high, gather))
    table[...] = equiv * gain_ext[...]

    group_done(group_recv, 0, lists, others)
    base = obs_tile - TABLE_PAD * LANES
    for start in range(0, members, 4):
        slots = jnp.concatenate([lists[start + i] for i in range(4)], axis=0) - base
        found = lookup(
            table, first_line, last_line, slots // LANES, slots & (LANES - 1)
        )
        for i in range(4):
            pick_out[start + i] = found[2 * i : 2 * i + 2, :]
    pick_in[me] = pick_out[me]
    to_group(1, lambda peer: pick_out.at[peer], pick_in.at[me])

    slab = 8 * lane_tiles
    for field in range(4):
        for at in range(lane_tiles):
            for row in range(2):
                slab_out[pl.ds(at * 8 + field * 2 + row, members, stride=slab), :] = work[
                    field, at, pl.ds(GUARD + HALO + row, members, stride=2), :
                ]
    own_slab = pl.ds(pl.multiple_of(me * slab, slab), slab)
    slab_in[own_slab, :] = slab_out[own_slab, :]
    to_group(
        2,
        lambda peer: slab_out.at[pl.ds(pl.multiple_of(peer * slab, slab), slab)],
        slab_in.at[own_slab],
    )

    names = jnp.concatenate([own_list] * 4, axis=0)
    slots = names - base
    high, low = slots // LANES, slots & (LANES - 1)
    value = lookup(value_ext, first_line, last_line, high, low)
    error = lookup(error_ext, first_line, last_line, high, low)
    value, error = value[0:2], error[0:2]
    row_index = me * 2 + iota((2, LANES), 0)
    centre = obs_tile + row_index * 64
    dist = (own_list - centre).astype(F32) / radius
    counts = count_ref[...]
    slot = iota((1, LANES), 1) & 63
    limit = jnp.concatenate(
        [
            jnp.where(
                left_half, counts[0:1, 2 * i : 2 * i + 1], counts[0:1, 2 * i + 1 : 2 * i + 2]
            )
            for i in range(2)
        ],
        axis=0,
    )
    live = slot < limit
    precision = jnp.where(live, 1.0 / ((1.0 + 4.0 * dist * dist) * error), 0.0)

    group_done(group_recv, 1, pick_in, others)
    size = 4 * members
    weighted, spreads, innovations = [], [], []
    for i in range(2):
        picked = pick_in[:, i, :]
        mean_eq = jnp.sum(picked, axis=0, keepdims=True) * (1.0 / members)
        spread = picked - mean_eq
        weighted.append(spread * precision[i : i + 1])
        spreads.append(spread)
        innovations.append(value[i : i + 1] - mean_eq)
    block_row = iota((size, LANES), 0) // members
    halves = (iota((size, LANES), 1) // 64 == block_row % 2, block_row // 2)

    def blocks(parts):
        return jnp.concatenate(
            [
                jnp.where(
                    jnp.logical_and(halves[0], halves[1] == i),
                    jnp.concatenate([parts[i]] * 4, axis=0),
                    0.0,
                )
                for i in range(2)
            ],
            axis=1,
        )

    weighted = blocks(weighted)
    spread = blocks(spreads)
    gram = lax.dot_general(
        weighted, spread, (((1,), (1,)), ((), ())), precision=HIGH, preferred_element_type=F32
    )
    proj = jnp.sum(weighted * jnp.concatenate(innovations, axis=1), axis=1, keepdims=True)

    line, column = iota((size, size), 0), iota((size, size), 1)
    diagonal = line == column
    same = line // members == column // members
    eye = jnp.where(diagonal, 1.0, 0.0)
    amat = gram + (members - 1.0) * eye
    trace = jnp.sum(jnp.where(diagonal, amat, 0.0), axis=1, keepdims=True)
    trace = jnp.concatenate(
        [
            jnp.broadcast_to(
                jnp.sum(trace[i * members : (i + 1) * members], axis=0, keepdims=True),
                (members, 1),
            )
            for i in range(4)
        ],
        axis=0,
    )

    def sweep(step, carry):
        current, inverse = carry
        factor = 1.5 * eye - 0.5 * dot3(inverse, current)
        return dot3(current, factor), dot3(factor, inverse)

    current, inverse = lax.fori_loop(0, NS_ITERS, sweep, (amat / trace, eye))
    root = inverse / jnp.sqrt(trace)
    wbar = dot3(root, dot3(root, jnp.broadcast_to(proj, (size, size))))
    wtot = jnp.where(same, (members - 1.0) ** 0.5 * root + wbar, 0.0)
    mean = jnp.sum(wtot, axis=0, keepdims=True) * (1.0 / members)
    mix = jnp.where(same, wtot - mean + 1.0 / members, 0.0)
    mix = jnp.transpose(mix)

    group_done(group_recv, 2, slab_in, others * slab)
    for field in range(4):
        for half in range(2):
            inputs = jnp.concatenate(
                [
                    jnp.concatenate(
                        [
                            slab_in[
                                pl.ds((side * 2 + half) * 8 + field * 2 + row, members, stride=slab), :
                            ]
                            for side in range(2)
                        ],
                        axis=0,
                    )
                    for row in range(2)
                ],
                axis=0,
            )
            mixed = dot3(mix, inputs)
            for row in range(2):
                for side in range(2):
                    patch = row * 2 + side
                    mix_out[
                        pl.ds((side * 2 + half) * 8 + field * 2 + row, members, stride=slab), :
                    ] = mixed[patch * members : (patch + 1) * members]
    back_in[own_slab, :] = mix_out[own_slab, :]
    to_group(
        3,
        lambda peer: mix_out.at[pl.ds(pl.multiple_of(peer * slab, slab), slab)],
        back_in.at[own_slab],
    )
    group_done(group_recv, 3, back_in, others * slab)
    for field in range(4):
        for at in range(lane_tiles):
            for row in range(2):
                rows_out[field, at, pl.ds(row, members, stride=2), :] = back_in[
                    pl.ds(at * 8 + field * 2 + row, members, stride=slab), :
                ]
    for field in range(4):
        for at in range(lane_tiles):
            out_ref[0, field, :, at * LANES : (at + 1) * LANES] = rows_out[field, at]

    for copy in halos:
        copy.wait_send()
    group_done(group_send, 0, lists, others)
    group_done(group_send, 1, pick_out, others)
    group_done(group_send, 2, slab_out, others * slab)
    group_done(group_send, 3, mix_out, others * slab)


def body(
    realization_array,
    water_depth,
    wet_mask,
    obs_cell,
    obs_value,
    obs_error,
    celer_gain,
    obs_list,
    obs_count,
):
    members = lax.axis_size("member")
    tiles = lax.axis_size("tile")
    grid_rows, width = water_depth.shape
    ext_rows = grid_rows + 2 * HALO
    lane_tiles = width // LANES
    own_table = obs_cell.shape[0] // LANES
    table_rows = own_table + 2 * TABLE_PAD
    slab_rows = members * 8 * lane_tiles
    deep = ext_rows + 2 * GUARD
    as_lines = lambda array: array.reshape(own_table, LANES)
    far = pl.BlockSpec(memory_space=pl.ANY)
    near = pl.BlockSpec(memory_space=pltpu.VMEM)
    return pl.pallas_call(
        functools.partial(kernel, members, tiles, grid_rows),
        out_shape=jax.ShapeDtypeStruct(realization_array.shape, F32),
        in_specs=[far] * 7 + [near] * 2,
        out_specs=near,
        scratch_shapes=[
            pltpu.VMEM((4, ext_rows, width), F32),
            pltpu.VMEM((ext_rows, width), F32),
            pltpu.VMEM((ext_rows, width), jnp.int32),
            pltpu.VMEM((table_rows, LANES), jnp.int32),
            pltpu.VMEM((table_rows, LANES), F32),
            pltpu.VMEM((table_rows, LANES), F32),
            pltpu.VMEM((table_rows, LANES), F32),
            pltpu.VMEM((4, lane_tiles, deep, LANES), F32),
            pltpu.VMEM((lane_tiles, deep, LANES), F32),
            pltpu.VMEM((lane_tiles, deep, LANES), F32),
            pltpu.VMEM((lane_tiles, deep, LANES), F32),
            pltpu.VMEM((lane_tiles, deep, LANES), F32),
            pltpu.VMEM((8, LANES), jnp.int32),
            pltpu.VMEM((members, 2, LANES), jnp.int32),
            pltpu.VMEM((table_rows, LANES), F32),
            pltpu.VMEM((members, 2, LANES), F32),
            pltpu.VMEM((members, 2, LANES), F32),
            pltpu.VMEM((slab_rows, LANES), F32),
            pltpu.VMEM((slab_rows, LANES), F32),
            pltpu.VMEM((slab_rows, LANES), F32),
            pltpu.VMEM((slab_rows, LANES), F32),
            pltpu.VMEM((4, lane_tiles, grid_rows, LANES), F32),
            pltpu.SemaphoreType.DMA((7,)),
            pltpu.SemaphoreType.DMA((2, 7)),
            pltpu.SemaphoreType.DMA((2, 7)),
            pltpu.SemaphoreType.DMA((4,)),
            pltpu.SemaphoreType.DMA((4,)),
        ],
        compiler_params=pltpu.CompilerParams(
            collective_id=0, has_side_effects=True, vmem_limit_bytes=32 * 1024 * 1024
        ),
    )(
        realization_array,
        water_depth,
        wet_mask,
        as_lines(obs_cell),
        as_lines(celer_gain),
        as_lines(obs_value),
        as_lines(obs_error),
        obs_list,
        obs_count,
    )


def solution(mesh):
    return jax.shard_map(
        body,
        mesh=mesh,
        in_specs=(
            P("member", None, "tile", None),
            P("tile", None),
            P("tile", None),
            P("tile"),
            P("tile"),
            P("tile"),
            P("tile"),
            P("tile", "member", None),
            P("tile", "member"),
        ),
        out_specs=P("member", None, "tile", None),
        check_vma=False,
    )
```

time: 428 us -> 57.4 us (0.13)
  other arithmetic: 161 us -> 0 us
  local copies, waits for them, and re-layouts: 112 us -> 7.19 us
  starting transfers between devices: 72.3 us -> 0 us
  blocking collectives: 63.5 us -> 0 us
  Pallas kernels: 0 us -> 49.3 us
  matrix products: 9.54 us -> 0 us
    unnamed x1 -> x0, other arithmetic: 147 us -> none
    ppermute x18 -> x0, starting transfers between devices: 66.1 us -> none  [the longest x9 39.8 us: padded_2(): lax.ppermute(lax.slice_in_dim(block, block.shape[dim] - width, None, axis...]
    pallas_call x0 -> x1, Pallas kernels: none -> 49.3 us  [body(): pl.pallas_call(functools.partial(kernel, members, tiles, grid_rows), out_...]
    all_gather x1 -> x0, blocking collectives: 41 us -> none  [body(): all_equiv = lax.all_gather(equiv[None], 'member', axis=0, tiled=True)]
    unnamed x15 -> x19, local copies, waits for them, and re-layouts: 46.7 us -> 7.19 us
    gather x7 -> x0, local copies, waits for them, and re-layouts: 27.5 us -> none  [the longest x1 23 us: body(): equiv = celer_gain * water_elevation.reshape(-1)[obs_cell]]
    another operation x5 -> x0, local copies, waits for them, and re-layouts: 24.5 us -> none  [body(): jnp.stack([water_elevation, eastward_velocity, northward_velocity, swell_...]
    all_to_all x1 -> x0, blocking collectives: 22.5 us -> none  [body(): lax.all_to_all(mixed.reshape(realization_pile, fields, per_dev * REGION_P...]
  transfers between devices with their start and end apart: 19 -> 0, of which waited for: 6 -> 0; matrix products, arithmetic and copies ran while one was open for 48% -> 0% of each run, Pallas kernels for 0% -> 0%
where the time goes in v1:
time: 57.4 us; the launch traced here: 56.5 us
  Pallas kernels  49.3 us (86%)
  local copies, waits for them, and re-layouts  7.19 us (13%)
    pallas_call x1, Pallas kernels, body(): pl.pallas_call(functools.partial(kernel, members, tiles, grid_rows), out_...  49.3 us
    unnamed x19, local copies, waits for them, and re-layouts  7.19 us

profile of v1, /device:TPU:5, one launch (start us, length us, event | category | flops | bytes accessed | tf_op | source)
XLA Modules:
  0.0 56.5 jit_solution(8909537526286689083)
XLA Ops:
  0.0 0.0 copy-start.7
  0.0 0.0 copy-start.8
  0.0 0.7 %copy-done.7 = s32[1,4,64]{2,1,0:T(4,128)S(1)} copy-done((s32[1,4,64]{2,1,0:T(4,128)S(1)}, s32[1,4,64]{2,1,0:T(4,128)}, u32[]{:S(2)}) %copy-start.7) | copy-done | bytes 1048
  0.7 0.0 copy-done.8
  0.7 0.0 copy-start
  0.7 1.0 %copy-done = f32[1,4,64,512]{3,2,1,0:T(8,128)S(1)} copy-done((f32[1,4,64,512]{3,2,1,0:T(8,128)S(1)}, f32[1,4,64,512]{3,2,1,0:T(8,128)}, u32[]{:S(2)}) %copy-start) | copy-done | bytes 524312
  1.7 0.0 copy-start.1
  1.7 0.9 %copy-done.1 = f32[64,512]{1,0:T(8,128)S(1)} copy-done((f32[64,512]{1,0:T(8,128)S(1)}, f32[64,512]{1,0:T(8,128)}, u32[]{:S(2)}) %copy-start.1) | copy-done | bytes 131096
  2.6 0.0 copy-start.2
  2.6 0.9 %copy-done.2 = s32[64,512]{1,0:T(8,128)S(1)} copy-done((s32[64,512]{1,0:T(8,128)S(1)}, s32[64,512]{1,0:T(8,128)}, u32[]{:S(2)}) %copy-start.2) | copy-done | bytes 131096
  3.5 0.0 copy-start.3
  3.5 0.7 %copy-done.3 = s32[4096]{0:T(1024)S(1)} copy-done((s32[4096]{0:T(1024)S(1)}, s32[4096]{0:T(1024)}, u32[]{:S(2)}) %copy-start.3) | copy-done | bytes 16408
  4.3 0.0 copy-start.4
  4.3 0.7 %copy-done.4 = f32[4096]{0:T(1024)S(1)} copy-done((f32[4096]{0:T(1024)S(1)}, f32[4096]{0:T(1024)}, u32[]{:S(2)}) %copy-start.4) | copy-done | bytes 16408
  5.0 0.0 copy-start.5
  5.0 0.7 %copy-done.5 = f32[4096]{0:T(1024)S(1)} copy-done((f32[4096]{0:T(1024)S(1)}, f32[4096]{0:T(1024)}, u32[]{:S(2)}) %copy-start.5) | copy-done | bytes 16408
  5.7 0.0 copy-start.6
  5.7 0.7 %copy-done.6 = f32[4096]{0:T(1024)S(1)} copy-done((f32[4096]{0:T(1024)S(1)}, f32[4096]{0:T(1024)}, u32[]{:S(2)}) %copy-start.6) | copy-done | bytes 16408
  6.4 49.3 %shard_map.91 = f32[1,4,64,512]{3,2,1,0:T(8,128)S(1)} custom-call(f32[1,4,64,512]{3,2,1,0:T(8,128)S(1)} %copy-done, f32[64,512]{1,0:T(8,128)S(1)} %copy-done.1, s32[64,512]{1,0:T(8,128)S(1)} %copy-done.2, s32[32,128]{1,0:T(8,128)S(1)} %bitcast.4, f32[32,128]{1,0:T(8,128)S(1)} %bitcast.5, f32[32,128]{1,0:T(8,128)S(1)} %bitcast.6, f32[32,128]{1,0:T(8,128)S(1)} %bitcast.7, ...), custom_call_target="tpu_custom_call" | custom-call | tf_op jit(solution)/shard_map/pallas_call | solution.py:499
  55.7 0.8 %copy.11 = f32[1,4,64,512]{3,2,1,0:T(8,128)} copy(f32[1,4,64,512]{3,2,1,0:T(8,128)S(1)} %shard_map.91) | data formatting | bytes 1048576
Async XLA Ops:
  0.0 0.7 %copy-start.7 = (s32[1,4,64]{2,1,0:T(4,128)S(1)}, s32[1,4,64]{2,1,0:T(4,128)}, u32[]{:S(2)}) copy-start(s32[1,4,64]{2,1,0:T(4,128)} %list_ref.1) | copy-start | bytes 3076
  0.0 0.7 %copy-start.8 = (s32[1,4]{1,0:T(1,128)S(1)}, s32[1,4]{1,0:T(1,128)}, u32[]{:S(2)}) copy-start(s32[1,4]{1,0:T(1,128)} %count_ref.1) | copy-start | bytes 52
  0.7 1.0 %copy-start = (f32[1,4,64,512]{3,2,1,0:T(8,128)S(1)}, f32[1,4,64,512]{3,2,1,0:T(8,128)}, u32[]{:S(2)}) copy-start(f32[1,4,64,512]{3,2,1,0:T(8,128)} %state_ref.1) | copy-start | bytes 1572868
  1.7 0.9 %copy-start.1 = (f32[64,512]{1,0:T(8,128)S(1)}, f32[64,512]{1,0:T(8,128)}, u32[]{:S(2)}) copy-start(f32[64,512]{1,0:T(8,128)} %depth_ref.1) | copy-start | bytes 393220
  2.6 0.9 %copy-start.2 = (s32[64,512]{1,0:T(8,128)S(1)}, s32[64,512]{1,0:T(8,128)}, u32[]{:S(2)}) copy-start(s32[64,512]{1,0:T(8,128)} %wet_ref.1) | copy-start | bytes 393220
  3.5 0.7 %copy-start.3 = (s32[4096]{0:T(1024)S(1)}, s32[4096]{0:T(1024)}, u32[]{:S(2)}) copy-start(s32[4096]{0:T(1024)} %param.12) | copy-start | bytes 49156
  4.3 0.7 %copy-start.4 = (f32[4096]{0:T(1024)S(1)}, f32[4096]{0:T(1024)}, u32[]{:S(2)}) copy-start(f32[4096]{0:T(1024)} %param.15) | copy-start | bytes 49156
  5.0 0.7 %copy-start.5 = (f32[4096]{0:T(1024)S(1)}, f32[4096]{0:T(1024)}, u32[]{:S(2)}) copy-start(f32[4096]{0:T(1024)} %param.13) | copy-start | bytes 49156
  5.7 0.7 %copy-start.6 = (f32[4096]{0:T(1024)S(1)}, f32[4096]{0:T(1024)}, u32[]{:S(2)}) copy-start(f32[4096]{0:T(1024)} %param.14) | copy-start | bytes 49156

commit v2 on v1

v2 whole, which is shorter than its diff:
```python
import functools

import jax
import jax.numpy as jnp
from jax import lax
from jax.experimental import pallas as pl
from jax.experimental.pallas import tpu as pltpu
from jax.sharding import PartitionSpec as P

MESH = pl.DeviceIdType.MESH
HIGH = lax.Precision.HIGHEST
F32 = jnp.float32
BF16 = jnp.bfloat16

REGION_POINTS = 256
STEPS = 4
NS_ITERS = 14
SPACING = 8

FRICTION = 0.98
PRESSURE = 0.25
DIVERGE = 0.25
FORCING = 0.05
UPWIND = 0.4
DAMPING = 0.02

LANES = 128
GUARD = 8
HALO = 16
OBS_HALO = 8
TABLE_PAD = 8


def iota(shape, dim):
    return lax.broadcasted_iota(jnp.int32, shape, dim)


def dot(left, right, precision=None):
    return lax.dot_general(
        left, right, (((1,), (0,)), ((), ())), precision=precision, preferred_element_type=F32
    )


def split(x):
    high = x.astype(BF16)
    return high, (x - high.astype(F32)).astype(BF16)


def dot3(left, right):
    left_high, left_low = split(left)
    right_high, right_low = split(right)
    rows = left.shape[0]
    both = dot(jnp.concatenate([left_high, left_low], axis=0), right_high)
    return (both[rows:] + dot(left_high, right_low)) + both[:rows]


def exact_dot(left, ones):
    high, _ = split(left)
    middle, low = split(left - high.astype(F32))
    rows = left.shape[0]
    parts = dot(jnp.concatenate([high, middle, low], axis=0), ones)
    return (parts[2 * rows :] + parts[rows : 2 * rows]) + parts[:rows]


def lookup(table, first, last, high, low):
    found = jnp.zeros(high.shape, table.dtype)
    for row in range(first, last):
        line = jnp.broadcast_to(table[row : row + 1, :], high.shape)
        found = jnp.where(
            high == row,
            jnp.take_along_axis(line, low, axis=1, mode="promise_in_bounds"),
            found,
        )
    return found


def kernel(
    members,
    tiles,
    grid_rows,
    state_ref,
    depth_ref,
    wet_ref,
    cell_ref,
    gain_ref,
    value_ref,
    error_ref,
    list_ref,
    count_ref,
    out_ref,
    state_ext,
    depth_ext,
    wet_ext,
    cell_ext,
    gain_ext,
    value_ext,
    error_ext,
    work,
    edge,
    hwork,
    wwork,
    flux,
    cross,
    edge_flux,
    edge_cross,
    raw_list,
    raw_count,
    pack,
    lists,
    table,
    pick_out,
    pick_in,
    slab_out,
    slab_in,
    mix_out,
    back_in,
    rows_out,
    local_sem,
    halo_send,
    halo_recv,
    group_send,
    group_recv,
):
    me = lax.axis_index("member")
    tile = lax.axis_index("tile")
    above = lax.rem(tile + tiles - 1, tiles)
    below = lax.rem(tile + 1, tiles)
    ext_rows = grid_rows + 2 * HALO
    lane_tiles = 4
    obs_tile = grid_rows * 64
    radius = obs_tile // 8
    own_table = obs_tile // LANES
    table_rows = own_table + 2 * TABLE_PAD
    others = members - 1

    barrier = pltpu.get_barrier_semaphore()

    def greet(step, carry):
        peer = lax.rem(me + step, members)
        pl.semaphore_signal(barrier, inc=1, device_id={"member": peer}, device_id_type=MESH)
        return carry

    pl.semaphore_signal(barrier, inc=1, device_id={"tile": above}, device_id_type=MESH)
    pl.semaphore_signal(barrier, inc=1, device_id={"tile": below}, device_id_type=MESH)
    lax.fori_loop(1, members, greet, 0)

    own_rows = pl.ds(HALO, grid_rows)
    own_lines = pl.ds(TABLE_PAD, own_table)
    tables = (
        (cell_ref, cell_ext),
        (gain_ref, gain_ext),
        (value_ref, value_ext),
        (error_ref, error_ext),
    )
    pairs = [
        (list_ref.at[0], raw_list),
        (count_ref, raw_count),
        (state_ref.at[0], state_ext.at[:, own_rows]),
        (depth_ref, depth_ext.at[own_rows]),
        (wet_ref, wet_ext.at[own_rows]),
    ] + [(ref, ext.at[own_lines]) for ref, ext in tables]
    local = [
        pltpu.make_async_copy(source, destination, local_sem.at[i])
        for i, (source, destination) in enumerate(pairs)
    ]
    for copy in local:
        copy.start()

    nothing = jnp.zeros((8, LANES), F32)
    strip = 2 * HALO
    own_start = GUARD + HALO
    own_end = own_start + grid_rows
    for at in range(lane_tiles):
        for field in (0, 3):
            work[field, at, own_start - 8 : own_start, :] = nothing
            work[field, at, own_end : own_end + 8, :] = nothing
            for side in range(2):
                edge[side, field, at, 0:GUARD, :] = nothing
                edge[side, field, at, GUARD + strip :, :] = nothing
        flux[at, own_start - 8 : own_start, :] = nothing
        flux[at, own_end : own_end + 8, :] = nothing
        for side in range(2):
            edge_flux[side, at, 0:GUARD, :] = nothing
            edge_flux[side, at, GUARD + strip :, :] = nothing
    pack[...] = jnp.zeros(pack.shape, jnp.int32)

    pl.semaphore_wait(barrier, others + 2)

    halos = []
    for way, (target, source_row, target_row, source_line, target_line) in enumerate(
        (
            (below, grid_rows - HALO, 0, own_table - TABLE_PAD, 0),
            (above, 0, HALO + grid_rows, 0, TABLE_PAD + own_table),
        )
    ):
        source_rows, target_rows = pl.ds(source_row, HALO), pl.ds(target_row, HALO)
        source_lines, target_lines = pl.ds(source_line, TABLE_PAD), pl.ds(target_line, TABLE_PAD)
        pairs = [
            (state_ref.at[0, :, source_rows], state_ext.at[:, target_rows]),
            (depth_ref.at[source_rows], depth_ext.at[target_rows]),
            (wet_ref.at[source_rows], wet_ext.at[target_rows]),
        ] + [(ref.at[source_lines], ext.at[target_lines]) for ref, ext in tables]
        for i, (source, destination) in enumerate(pairs):
            copy = pltpu.make_async_remote_copy(
                src_ref=source,
                dst_ref=destination,
                send_sem=halo_send.at[way, i],
                recv_sem=halo_recv.at[way, i],
                device_id={"tile": target},
                device_id_type=MESH,
            )
            copy.start()
            halos.append(copy)

    def send(which, peer, source, destination):
        pltpu.make_async_remote_copy(
            src_ref=source,
            dst_ref=destination,
            send_sem=group_send.at[which],
            recv_sem=group_recv.at[which],
            device_id={"member": peer},
            device_id_type=MESH,
        ).start()

    def to_group(which, source, destination):
        def one(step, carry):
            peer = lax.rem(me + step, members)
            send(which, peer, source(peer), destination)
            return carry

        lax.fori_loop(1, members, one, 0)

    def group_done(sems, which, ref, size):
        part = ref.at[pl.ds(0, size)]
        pltpu.make_async_copy(part, part, sems.at[which]).wait()

    local[0].wait()
    pack[0:4, 0:64] = raw_list[...]
    packed = pack[...]
    turned = pltpu.roll(packed, 64, axis=1)
    left_half = iota((1, LANES), 1) < 64
    own_list = jnp.concatenate(
        [
            jnp.where(left_half, packed[0:1], turned[1:2]),
            jnp.where(left_half, packed[2:3], turned[3:4]),
        ],
        axis=0,
    )
    lists[me] = own_list
    to_group(0, lambda peer: lists.at[me], lists.at[me])
    for copy in local[1:]:
        copy.wait()

    def unpack(start, inside, targets):
        rows = slice(start, start + 8)
        put = slice(GUARD + start, GUARD + start + 8)
        for at in range(lane_tiles):
            lanes = slice(at * LANES, (at + 1) * LANES)
            parts = [state_ext[field, rows, lanes] for field in range(4)]
            if inside is not None:
                parts = [jnp.where(inside, part, 0.0) for part in parts]
            for target, target_rows in targets:
                for field in range(4):
                    target[field, at, target_rows, :] = parts[field]
            wet = wet_ext[rows, lanes].astype(F32)
            if inside is not None:
                wet = jnp.where(inside, wet, 0.0)
            wwork[at, put, :] = wet
            hwork[at, put, :] = depth_ext[rows, lanes]

    edge_starts = (0, ext_rows - strip)
    for start in range(HALO, HALO + grid_rows, 8):
        targets = [(work, slice(GUARD + start, GUARD + start + 8))]
        for side in range(2):
            at_row = start - edge_starts[side]
            if 0 <= at_row < strip:
                targets.append((edge.at[side], slice(GUARD + at_row, GUARD + at_row + 8)))
        unpack(start, None, targets)

    first_lane = iota((8, LANES), 1) == 0
    end_lane = iota((8, LANES), 1) == LANES - 1

    def across(parts):
        up = [pltpu.roll(part, LANES - 1, axis=1) for part in parts] + [nothing]
        down = [nothing] + [pltpu.roll(part, 1, axis=1) for part in parts]
        return [
            jnp.where(end_lane, up[at + 1], up[at])
            - jnp.where(first_lane, down[at], down[at + 1])
            for at in range(lane_tiles)
        ]

    def advance(fields, flux, cross, first, last, shift):
        for start in range(first, last, 8):
            rows = slice(start, start + 8)
            fixed = slice(start + shift, start + shift + 8)
            after = slice(start + 1, start + 9)
            before = slice(start - 1, start + 7)
            slope_y = across([fields[0, at, rows, :] for at in range(lane_tiles)])
            flow = []
            for at in range(lane_tiles):
                wet = wwork[at, fixed, :]
                height = hwork[at, fixed, :]
                slope_x = fields[0, at, after, :] - fields[0, at, before, :]
                new_x = wet * (FRICTION * fields[1, at, rows, :] - PRESSURE * slope_x)
                new_y = wet * (FRICTION * fields[2, at, rows, :] - PRESSURE * slope_y[at])
                fields[1, at, rows, :] = new_x
                fields[2, at, rows, :] = new_y
                flux[at, rows, :] = height * new_x
                flow.append(height * new_y)
            for at, part in enumerate(across(flow)):
                cross[at, rows, :] = part
        for start in range(last - 8, first - 8, -8):
            rows = slice(start, start + 8)
            fixed = slice(start + shift, start + shift + 8)
            after = slice(start + 1, start + 9)
            before = slice(start - 1, start + 7)
            for at in range(lane_tiles):
                wet = wwork[at, fixed, :]
                level = fields[0, at, rows, :]
                energy = fields[3, at, rows, :]
                spill = (flux[at, after, :] - flux[at, before, :]) + cross[at, rows, :]
                fields[0, at, rows, :] = wet * (level - DIVERGE * spill + FORCING * energy)
                fields[3, at, rows, :] = wet * (
                    energy - UPWIND * (energy - fields[3, at, before, :]) - DAMPING * energy
                )

    def inner_step(step, carry):
        advance(work, flux, cross, own_start, own_end, 0)
        return carry

    lax.fori_loop(0, STEPS, inner_step, 0)

    slab = 4 * lane_tiles
    edge_owners = HALO // 4

    def build(chunk, first, last):
        for field in range(2):
            for at in range(lane_tiles):
                for row in range(2):
                    slab_out[
                        chunk,
                        pl.ds(
                            first * slab + field * 8 + at * 2 + row, last - first, stride=slab
                        ),
                        :,
                    ] = work[
                        2 * chunk + field,
                        at,
                        pl.ds(own_start + 2 * first + row, last - first, stride=2),
                        :,
                    ]

    def slab_of(ref, chunk, owner):
        return ref.at[chunk, pl.ds(pl.multiple_of(owner * slab, slab), slab)]

    def send_slabs(chunk, first, last):
        count = last - first

        def one(step, carry):
            peer = first + lax.rem(me + step, count)

            @pl.when(peer != me)
            def _():
                send(2 + chunk, peer, slab_of(slab_out, chunk, peer), slab_of(slab_in, chunk, me))

            return carry

        lax.fori_loop(0, count, one, 0)

    if members > 2 * edge_owners:
        for chunk in range(2):
            build(chunk, edge_owners, members - edge_owners)
        send_slabs(0, edge_owners, members - edge_owners)

    for copy in halos:
        copy.wait_recv()
    for start in range(0, HALO, 8):
        unpack(start, tile > 0, [(edge.at[0], slice(GUARD + start, GUARD + start + 8))])
    for start in range(HALO + grid_rows, ext_rows, 8):
        at_row = start - edge_starts[1]
        unpack(
            start,
            tile < tiles - 1,
            [(edge.at[1], slice(GUARD + at_row, GUARD + at_row + 8))],
        )

    def edge_step(step, carry):
        for side in range(2):
            advance(
                edge.at[side],
                edge_flux.at[side],
                edge_cross.at[side],
                GUARD,
                GUARD + strip,
                edge_starts[side],
            )
        return carry

    lax.fori_loop(0, STEPS, edge_step, 0)
    for side in range(2):
        for start in (GUARD + 8, GUARD + 16):
            for field in range(4):
                for at in range(lane_tiles):
                    put = start + edge_starts[side]
                    work[field, at, put : put + 8, :] = edge[side, field, at, start : start + 8, :]

    first_line = TABLE_PAD - OBS_HALO // 2
    last_line = TABLE_PAD + own_table + OBS_HALO // 2
    offset = (cell_ext[...] & (SPACING - 1)).astype(BF16)
    place = iota((1, LANES), 1) & (SPACING - 1)
    chosen = [[], [], []]
    gathers = []
    for parity in range(2):
        for at in range(lane_tiles):
            owner = iota((LANES, LANES), 0) // SPACING + (parity * 64 + at * 16)
            gathers.append((owner == iota((LANES, LANES), 1)).astype(BF16))
            owner_t = iota((LANES, LANES), 1) // SPACING + (parity * 64 + at * 16)
            scatter = (owner_t == iota((LANES, LANES), 0)).astype(BF16)
            wanted = dot(offset, scatter).astype(jnp.int32) == place
            level = work[0, at, pl.ds(GUARD + parity, table_rows, stride=2), :]
            level = jnp.where(wanted, level, 0.0)
            high, _ = split(level)
            middle, low = split(level - high.astype(F32))
            for part, piece in zip(chosen, (high, middle, low)):
                part.append(piece)
    gather = jnp.concatenate(gathers, axis=0)
    pieces = [dot(jnp.concatenate(part, axis=1), gather) for part in chosen]
    table[...] = ((pieces[2] + pieces[1]) + pieces[0]) * gain_ext[...]

    group_done(group_recv, 0, lists, others)
    base = obs_tile - TABLE_PAD * LANES
    for start in range(0, members, 4):
        slots = jnp.concatenate([lists[start + i] for i in range(4)], axis=0) - base
        found = lookup(
            table, first_line, last_line, slots // LANES, slots & (LANES - 1)
        )
        for i in range(4):
            pick_out[start + i] = found[2 * i : 2 * i + 2, :]
    pick_in[me] = pick_out[me]
    to_group(1, lambda peer: pick_out.at[peer], pick_in.at[me])

    for chunk in range(2):
        build(chunk, 0, edge_owners)
        build(chunk, members - edge_owners, members)
    send_slabs(0, 0, edge_owners)
    send_slabs(0, members - edge_owners, members)
    send_slabs(1, 0, members)
    own_slab = pl.ds(pl.multiple_of(me * slab, slab), slab)
    for chunk in range(2):
        slab_in[chunk, own_slab, :] = slab_out[chunk, own_slab, :]

    names = jnp.concatenate([own_list] * 4, axis=0)
    slots = names - base
    high, low = slots // LANES, slots & (LANES - 1)
    value = lookup(value_ext, first_line, last_line, high, low)
    error = lookup(error_ext, first_line, last_line, high, low)
    value, error = value[0:2], error[0:2]
    row_index = me * 2 + iota((2, LANES), 0)
    centre = obs_tile + row_index * 64
    dist = (own_list - centre).astype(F32) / radius
    counts = raw_count[...]
    slot = iota((1, LANES), 1) & 63
    limit = jnp.concatenate(
        [
            jnp.where(
                left_half, counts[0:1, 2 * i : 2 * i + 1], counts[0:1, 2 * i + 1 : 2 * i + 2]
            )
            for i in range(2)
        ],
        axis=0,
    )
    live = slot < limit
    precision = jnp.where(live, 1.0 / ((1.0 + 4.0 * dist * dist) * error), 0.0)

    size = 4 * members
    patch_of_line = iota((size, 2 * LANES), 0) // members
    patch_of_slot = iota((size, 2 * LANES), 1) // 64
    line, column = iota((size, size), 0) // members, iota((size, size), 1) // members
    same = line == column
    diagonal = iota((members, size), 0) == iota((members, size), 1) % members
    eye = jnp.where(diagonal, 1.0, 0.0)
    ones = jnp.where(same, 1.0, 0.0).astype(BF16)
    patch_ones = (iota((2 * LANES, size), 0) // 64 == iota((2 * LANES, size), 1) // members)
    patch_ones = jnp.where(patch_ones, 1.0, 0.0).astype(BF16)

    def blocks(packed):
        return jnp.where(same, jnp.concatenate([packed] * 4, axis=0), 0.0)

    group_done(group_recv, 1, pick_in, others)
    picked = jnp.concatenate([pick_in[:, i, :] for i in range(2)], axis=1)
    mean_eq = jnp.sum(picked, axis=0, keepdims=True) * (1.0 / members)
    spread = picked - mean_eq
    precision = jnp.concatenate([precision[0:1], precision[1:2]], axis=1)
    value = jnp.concatenate([value[0:1], value[1:2]], axis=1)
    weighted = spread * precision
    by_patch = jnp.where(
        patch_of_line == patch_of_slot, jnp.concatenate([spread] * 4, axis=0), 0.0
    )
    gram = lax.dot_general(
        weighted, by_patch, (((1,), (1,)), ((), ())), precision=HIGH, preferred_element_type=F32
    )
    proj = exact_dot(weighted * (value - mean_eq), patch_ones)

    amat = gram + (members - 1.0) * eye
    trace = jnp.sum(exact_dot(jnp.where(diagonal, amat, 0.0), ones), axis=0, keepdims=True)

    def sweep(step, carry):
        current, inverse = carry
        factor = 1.5 * eye - 0.5 * dot3(inverse, blocks(current))
        return dot3(current, blocks(factor)), dot3(factor, blocks(inverse))

    current, inverse = lax.fori_loop(0, NS_ITERS, sweep, (amat / trace, eye))
    root = inverse / jnp.sqrt(trace)
    wbar = dot3(root, blocks(dot3(root, blocks(proj))))
    wtot = (members - 1.0) ** 0.5 * root + wbar
    mean = jnp.sum(wtot, axis=0, keepdims=True) * (1.0 / members)
    mix = jnp.transpose(blocks(wtot - mean + 1.0 / members))
    mix_high, mix_low = split(mix)
    mix_both = jnp.concatenate([mix_high, mix_low], axis=0)

    for chunk in range(2):
        group_done(group_recv, 2 + chunk, slab_in.at[chunk], others * slab)
        for field in range(2):
            lines = [
                [
                    slab_in[chunk, pl.ds(field * 8 + at * 2 + row, members, stride=slab), :]
                    for at in range(lane_tiles)
                ]
                for row in range(2)
            ]
            inputs = jnp.concatenate(
                [
                    jnp.concatenate(lines[row][2 * side : 2 * side + 2], axis=1)
                    for row in range(2)
                    for side in range(2)
                ],
                axis=0,
            )
            high, low = split(inputs)
            both = dot(mix_both, high)
            mixed = (both[size:] + dot(mix_high, low)) + both[:size]
            for row in range(2):
                for at in range(lane_tiles):
                    patch = row * 2 + at // 2
                    mix_out[
                        chunk, pl.ds(field * 8 + at * 2 + row, members, stride=slab), :
                    ] = mixed[
                        patch * members : (patch + 1) * members,
                        (at % 2) * LANES : (at % 2 + 1) * LANES,
                    ]
        back_in[chunk, own_slab, :] = mix_out[chunk, own_slab, :]
        to_group(
            4 + chunk,
            lambda peer: slab_of(mix_out, chunk, peer),
            back_in.at[chunk, own_slab],
        )
    for chunk in range(2):
        group_done(group_recv, 4 + chunk, back_in.at[chunk], others * slab)
        for field in range(2):
            for at in range(lane_tiles):
                for row in range(2):
                    rows_out[2 * chunk + field, at, pl.ds(row, members, stride=2), :] = back_in[
                        chunk, pl.ds(field * 8 + at * 2 + row, members, stride=slab), :
                    ]
        for field in range(2 * chunk, 2 * chunk + 2):
            for at in range(lane_tiles):
                out_ref[0, field, :, at * LANES : (at + 1) * LANES] = rows_out[field, at]

    for copy in halos:
        copy.wait_send()
    group_done(group_send, 0, lists, others)
    group_done(group_send, 1, pick_out, others)
    for chunk in range(2):
        group_done(group_send, 2 + chunk, slab_out.at[chunk], others * slab)
        group_done(group_send, 4 + chunk, mix_out.at[chunk], others * slab)


def body(
    realization_array,
    water_depth,
    wet_mask,
    obs_cell,
    obs_value,
    obs_error,
    celer_gain,
    obs_list,
    obs_count,
):
    members = lax.axis_size("member")
    tiles = lax.axis_size("tile")
    grid_rows, width = water_depth.shape
    ext_rows = grid_rows + 2 * HALO
    lane_tiles = width // LANES
    own_table = obs_cell.shape[0] // LANES
    table_rows = own_table + 2 * TABLE_PAD
    slab_rows = members * 4 * lane_tiles
    strip = 2 * HALO + 2 * GUARD
    deep = ext_rows + 2 * GUARD
    as_lines = lambda array: array.reshape(own_table, LANES)
    far = pl.BlockSpec(memory_space=pltpu.HBM)
    near = pl.BlockSpec(memory_space=pltpu.VMEM)
    return pl.pallas_call(
        functools.partial(kernel, members, tiles, grid_rows),
        out_shape=jax.ShapeDtypeStruct(realization_array.shape, F32),
        in_specs=[far] * 9,
        out_specs=near,
        scratch_shapes=[
            pltpu.VMEM((4, ext_rows, width), F32),
            pltpu.VMEM((ext_rows, width), F32),
            pltpu.VMEM((ext_rows, width), jnp.int32),
            pltpu.VMEM((table_rows, LANES), jnp.int32),
            pltpu.VMEM((table_rows, LANES), F32),
            pltpu.VMEM((table_rows, LANES), F32),
            pltpu.VMEM((table_rows, LANES), F32),
            pltpu.VMEM((4, lane_tiles, deep, LANES), F32),
            pltpu.VMEM((2, 4, lane_tiles, strip, LANES), F32),
            pltpu.VMEM((lane_tiles, deep, LANES), F32),
            pltpu.VMEM((lane_tiles, deep, LANES), F32),
            pltpu.VMEM((lane_tiles, deep, LANES), F32),
            pltpu.VMEM((lane_tiles, deep, LANES), F32),
            pltpu.VMEM((2, lane_tiles, strip, LANES), F32),
            pltpu.VMEM((2, lane_tiles, strip, LANES), F32),
            pltpu.VMEM(obs_list.shape[1:], jnp.int32),
            pltpu.VMEM(obs_count.shape, jnp.int32),
            pltpu.VMEM((8, LANES), jnp.int32),
            pltpu.VMEM((members, 2, LANES), jnp.int32),
            pltpu.VMEM((table_rows, LANES), F32),
            pltpu.VMEM((members, 2, LANES), F32),
            pltpu.VMEM((members, 2, LANES), F32),
            pltpu.VMEM((2, slab_rows, LANES), F32),
            pltpu.VMEM((2, slab_rows, LANES), F32),
            pltpu.VMEM((2, slab_rows, LANES), F32),
            pltpu.VMEM((2, slab_rows, LANES), F32),
            pltpu.VMEM((4, lane_tiles, grid_rows, LANES), F32),
            pltpu.SemaphoreType.DMA((9,)),
            pltpu.SemaphoreType.DMA((2, 7)),
            pltpu.SemaphoreType.DMA((2, 7)),
            pltpu.SemaphoreType.DMA((6,)),
            pltpu.SemaphoreType.DMA((6,)),
        ],
        compiler_params=pltpu.CompilerParams(
            collective_id=0, has_side_effects=True, vmem_limit_bytes=32 * 1024 * 1024
        ),
    )(
        *[
            pltpu.with_memory_space_constraint(array, pltpu.HBM)
            for array in (
                realization_array,
                water_depth,
                wet_mask,
                as_lines(obs_cell),
                as_lines(celer_gain),
                as_lines(obs_value),
                as_lines(obs_error),
                obs_list,
                obs_count,
            )
        ]
    )


def solution(mesh):
    return jax.shard_map(
        body,
        mesh=mesh,
        in_specs=(
            P("member", None, "tile", None),
            P("tile", None),
            P("tile", None),
            P("tile"),
            P("tile"),
            P("tile"),
            P("tile"),
            P("tile", "member", None),
            P("tile", "member"),
        ),
        out_specs=P("member", None, "tile", None),
        check_vma=False,
    )
```

time: 57.4 us -> 43 us (0.75); the launches traced: 56.5 us -> 43 us
  Pallas kernels: 49.3 us -> 42.1 us
  local copies, waits for them, and re-layouts: 7.19 us -> 0.8 us
    pallas_call x1, Pallas kernels: 49.3 us -> 42.1 us  [body(): pl.pallas_call(functools.partial(kernel, members, tiles, grid_rows), out_...]
    unnamed x19 -> x1, local copies, waits for them, and re-layouts: 7.19 us -> 0.8 us
where the time goes in v2:
time: 43 us
  Pallas kernels  42.1 us (98%)
  local copies, waits for them, and re-layouts  0.8 us (2%)
    pallas_call x1, Pallas kernels, body(): pl.pallas_call(functools.partial(kernel, members, tiles, grid_rows), out_...  42.1 us

profile of v2, /device:TPU:5, one launch (start us, length us, event | category | flops | bytes accessed | tf_op | source)
XLA Modules:
  0.0 43.0 jit_solution(577656256503059647)
XLA Ops:
  0.0 42.1 %shard_map.91 = f32[1,4,64,512]{3,2,1,0:T(8,128)S(1)} custom-call(f32[1,4,64,512]{3,2,1,0:T(8,128)} %state_ref.1, f32[64,512]{1,0:T(8,128)} %depth_ref.1, s32[64,512]{1,0:T(8,128)} %wet_ref.1, s32[32,128]{1,0:T(8,128)} %bitcast.4, f32[32,128]{1,0:T(8,128)} %bitcast.5, f32[32,128]{1,0:T(8,128)} %bitcast.6, f32[32,128]{1,0:T(8,128)} %bitcast.7, ...), custom_call_target="tpu_custom_call" | custom-call | tf_op jit(solution)/shard_map/pallas_call | solution.py:602
  42.2 0.8 %copy.11 = f32[1,4,64,512]{3,2,1,0:T(8,128)} copy(f32[1,4,64,512]{3,2,1,0:T(8,128)S(1)} %shard_map.91) | data formatting | bytes 1048576

commit v3 on v2

--- a/solution.py
+++ b/solution.py
@@ -13,6 +13,8 @@
 BF16 = jnp.bfloat16
 
 REGION_POINTS = 256
+OUTWARD = ((0, 1), (2, 3))
+BACK = ((0,), (1,), (2, 3))
 STEPS = 4
 NS_ITERS = 14
 SPACING = 8
@@ -46,19 +48,26 @@
     return high, (x - high.astype(F32)).astype(BF16)
 
 
-def dot3(left, right):
-    left_high, left_low = split(left)
-    right_high, right_low = split(right)
+def split3(x):
+    high, _ = split(x)
+    middle, low = split(x - high.astype(F32))
+    return high, middle, low
+
+
+def dot6(left, right):
+    left_high, left_middle, left_low = split3(left)
+    right_high, right_middle, right_low = split3(right)
     rows = left.shape[0]
-    both = dot(jnp.concatenate([left_high, left_low], axis=0), right_high)
-    return (both[rows:] + dot(left_high, right_low)) + both[:rows]
+    first = dot(jnp.concatenate([left_high, left_middle, left_low], axis=0), right_high)
+    second = dot(jnp.concatenate([left_high, left_middle], axis=0), right_middle)
+    third = dot(left_high, right_low)
+    small = first[2 * rows :] + second[rows:] + third
+    return (small + (first[rows : 2 * rows] + second[:rows])) + first[:rows]
 
 
 def exact_dot(left, ones):
-    high, _ = split(left)
-    middle, low = split(left - high.astype(F32))
     rows = left.shape[0]
-    parts = dot(jnp.concatenate([high, middle, low], axis=0), ones)
+    parts = dot(jnp.concatenate(split3(left), axis=0), ones)
     return (parts[2 * rows :] + parts[rows : 2 * rows]) + parts[:rows]
 
 
@@ -184,56 +193,6 @@
             edge_flux[side, at, GUARD + strip :, :] = nothing
     pack[...] = jnp.zeros(pack.shape, jnp.int32)
 
-    pl.semaphore_wait(barrier, others + 2)
-
-    halos = []
-    for way, (target, source_row, target_row, source_line, target_line) in enumerate(
-        (
-            (below, grid_rows - HALO, 0, own_table - TABLE_PAD, 0),
-            (above, 0, HALO + grid_rows, 0, TABLE_PAD + own_table),
-        )
-    ):
-        source_rows, target_rows = pl.ds(source_row, HALO), pl.ds(target_row, HALO)
-        source_lines, target_lines = pl.ds(source_line, TABLE_PAD), pl.ds(target_line, TABLE_PAD)
-        pairs = [
-            (state_ref.at[0, :, source_rows], state_ext.at[:, target_rows]),
-            (depth_ref.at[source_rows], depth_ext.at[target_rows]),
-            (wet_ref.at[source_rows], wet_ext.at[target_rows]),
-        ] + [(ref.at[source_lines], ext.at[target_lines]) for ref, ext in tables]
-        for i, (source, destination) in enumerate(pairs):
-            copy = pltpu.make_async_remote_copy(
-                src_ref=source,
-                dst_ref=destination,
-                send_sem=halo_send.at[way, i],
-                recv_sem=halo_recv.at[way, i],
-                device_id={"tile": target},
-                device_id_type=MESH,
-            )
-            copy.start()
-            halos.append(copy)
-
-    def send(which, peer, source, destination):
-        pltpu.make_async_remote_copy(
-            src_ref=source,
-            dst_ref=destination,
-            send_sem=group_send.at[which],
-            recv_sem=group_recv.at[which],
-            device_id={"member": peer},
-            device_id_type=MESH,
-        ).start()
-
-    def to_group(which, source, destination):
-        def one(step, carry):
-            peer = lax.rem(me + step, members)
-            send(which, peer, source(peer), destination)
-            return carry
-
-        lax.fori_loop(1, members, one, 0)
-
-    def group_done(sems, which, ref, size):
-        part = ref.at[pl.ds(0, size)]
-        pltpu.make_async_copy(part, part, sems.at[which]).wait()
-
     local[0].wait()
     pack[0:4, 0:64] = raw_list[...]
     packed = pack[...]
@@ -247,7 +206,6 @@
         axis=0,
     )
     lists[me] = own_list
-    to_group(0, lambda peer: lists.at[me], lists.at[me])
     for copy in local[1:]:
         copy.wait()
 
@@ -328,30 +286,79 @@
         advance(work, flux, cross, own_start, own_end, 0)
         return carry
 
+    pl.semaphore_wait(barrier, others + 2)
+
+    halos = []
+    for way, (target, source_row, target_row, source_line, target_line) in enumerate(
+        (
+            (below, grid_rows - HALO, 0, own_table - TABLE_PAD, 0),
+            (above, 0, HALO + grid_rows, 0, TABLE_PAD + own_table),
+        )
+    ):
+        source_rows, target_rows = pl.ds(source_row, HALO), pl.ds(target_row, HALO)
+        source_lines, target_lines = pl.ds(source_line, TABLE_PAD), pl.ds(target_line, TABLE_PAD)
+        pairs = [
+            (state_ref.at[0, :, source_rows], state_ext.at[:, target_rows]),
+            (depth_ref.at[source_rows], depth_ext.at[target_rows]),
+            (wet_ref.at[source_rows], wet_ext.at[target_rows]),
+        ] + [(ref.at[source_lines], ext.at[target_lines]) for ref, ext in tables]
+        for i, (source, destination) in enumerate(pairs):
+            copy = pltpu.make_async_remote_copy(
+                src_ref=source,
+                dst_ref=destination,
+                send_sem=halo_send.at[way, i],
+                recv_sem=halo_recv.at[way, i],
+                device_id={"tile": target},
+                device_id_type=MESH,
+            )
+            copy.start()
+            halos.append(copy)
+
+    def send(which, peer, source, destination):
+        pltpu.make_async_remote_copy(
+            src_ref=source,
+            dst_ref=destination,
+            send_sem=group_send.at[which],
+            recv_sem=group_recv.at[which],
+            device_id={"member": peer},
+            device_id_type=MESH,
+        ).start()
+
+    def to_group(which, source, destination):
+        def one(step, carry):
+            peer = lax.rem(me + step, members)
+            send(which, peer, source(peer), destination)
+            return carry
+
+        lax.fori_loop(1, members, one, 0)
+
+    def group_done(sems, which, ref, size):
+        part = ref.at[pl.ds(0, size)]
+        pltpu.make_async_copy(part, part, sems.at[which]).wait()
+
+    to_group(0, lambda peer: lists.at[me], lists.at[me])
     lax.fori_loop(0, STEPS, inner_step, 0)
 
-    slab = 4 * lane_tiles
+    slab = 2 * lane_tiles
     edge_owners = HALO // 4
 
-    def build(chunk, first, last):
-        for field in range(2):
-            for at in range(lane_tiles):
-                for row in range(2):
-                    slab_out[
-                        chunk,
-                        pl.ds(
-                            first * slab + field * 8 + at * 2 + row, last - first, stride=slab
-                        ),
-                        :,
-                    ] = work[
-                        2 * chunk + field,
-                        at,
-                        pl.ds(own_start + 2 * first + row, last - first, stride=2),
-                        :,
-                    ]
-
-    def slab_of(ref, chunk, owner):
-        return ref.at[chunk, pl.ds(pl.multiple_of(owner * slab, slab), slab)]
+    def build(field, first, last):
+        for at in range(lane_tiles):
+            for row in range(2):
+                slab_out[
+                    field, pl.ds(first * slab + at * 2 + row, last - first, stride=slab), :
+                ] = work[
+                    field, at, pl.ds(own_start + 2 * first + row, last - first, stride=2), :
+                ]
+
+    def slab_of(ref, fields, owner):
+        return ref.at[
+            pl.ds(fields[0], len(fields)), pl.ds(pl.multiple_of(owner * slab, slab), slab)
+        ]
+
+    def slabs_done(sems, which, ref, fields):
+        part = ref.at[pl.ds(fields[0], len(fields)), pl.ds(0, others * slab)]
+        pltpu.make_async_copy(part, part, sems.at[which]).wait()
 
     def send_slabs(chunk, first, last):
         count = last - first
@@ -361,15 +368,16 @@
 
             @pl.when(peer != me)
             def _():
-                send(2 + chunk, peer, slab_of(slab_out, chunk, peer), slab_of(slab_in, chunk, me))
+                fields = OUTWARD[chunk]
+                send(2 + chunk, peer, slab_of(slab_out, fields, peer), slab_of(slab_in, fields, me))
 
             return carry
 
         lax.fori_loop(0, count, one, 0)
 
     if members > 2 * edge_owners:
-        for chunk in range(2):
-            build(chunk, edge_owners, members - edge_owners)
+        for field in range(4):
+            build(field, edge_owners, members - edge_owners)
         send_slabs(0, edge_owners, members - edge_owners)
 
     for copy in halos:
@@ -419,9 +427,7 @@
             wanted = dot(offset, scatter).astype(jnp.int32) == place
             level = work[0, at, pl.ds(GUARD + parity, table_rows, stride=2), :]
             level = jnp.where(wanted, level, 0.0)
-            high, _ = split(level)
-            middle, low = split(level - high.astype(F32))
-            for part, piece in zip(chosen, (high, middle, low)):
+            for part, piece in zip(chosen, split3(level)):
                 part.append(piece)
     gather = jnp.concatenate(gathers, axis=0)
     pieces = [dot(jnp.concatenate(part, axis=1), gather) for part in chosen]
@@ -439,15 +445,15 @@
     pick_in[me] = pick_out[me]
     to_group(1, lambda peer: pick_out.at[peer], pick_in.at[me])
 
-    for chunk in range(2):
-        build(chunk, 0, edge_owners)
-        build(chunk, members - edge_owners, members)
+    for field in range(4):
+        build(field, 0, edge_owners)
+        build(field, members - edge_owners, members)
     send_slabs(0, 0, edge_owners)
     send_slabs(0, members - edge_owners, members)
     send_slabs(1, 0, members)
     own_slab = pl.ds(pl.multiple_of(me * slab, slab), slab)
-    for chunk in range(2):
-        slab_in[chunk, own_slab, :] = slab_out[chunk, own_slab, :]
+    for field in range(4):
+        slab_in[field, own_slab, :] = slab_out[field, own_slab, :]
 
     names = jnp.concatenate([own_list] * 4, axis=0)
     slots = names - base
@@ -479,7 +485,6 @@
     same = line == column
     diagonal = iota((members, size), 0) == iota((members, size), 1) % members
     eye = jnp.where(diagonal, 1.0, 0.0)
-    ones = jnp.where(same, 1.0, 0.0).astype(BF16)
     patch_ones = (iota((2 * LANES, size), 0) // 64 == iota((2 * LANES, size), 1) // members)
     patch_ones = jnp.where(patch_ones, 1.0, 0.0).astype(BF16)
 
@@ -499,31 +504,53 @@
     gram = lax.dot_general(
         weighted, by_patch, (((1,), (1,)), ((), ())), precision=HIGH, preferred_element_type=F32
     )
-    proj = exact_dot(weighted * (value - mean_eq), patch_ones)
+    sums = exact_dot(
+        jnp.concatenate([weighted * (value - mean_eq), weighted * spread], axis=0), patch_ones
+    )
+    proj = sums[:members]
+    trace = jnp.sum(sums[members:], axis=0, keepdims=True) + (members - 1.0) * members
 
     amat = gram + (members - 1.0) * eye
-    trace = jnp.sum(exact_dot(jnp.where(diagonal, amat, 0.0), ones), axis=0, keepdims=True)
-
-    def sweep(step, carry):
-        current, inverse = carry
-        factor = 1.5 * eye - 0.5 * dot3(inverse, blocks(current))
-        return dot3(current, blocks(factor)), dot3(factor, blocks(inverse))
-
-    current, inverse = lax.fori_loop(0, NS_ITERS, sweep, (amat / trace, eye))
-    root = inverse / jnp.sqrt(trace)
-    wbar = dot3(root, blocks(dot3(root, blocks(proj))))
-    wtot = (members - 1.0) ** 0.5 * root + wbar
+
+    def times(left, right):
+        return dot6(left, blocks(right))
+
+    def two_steps(square):
+        second = times(square, square)
+        third, fourth = times(second, square), times(second, second)
+        after = 2.25 * square - 1.5 * second + 0.25 * third
+        both = 2.25 * second - 1.5 * third + 0.25 * fourth
+        return second, 2.25 * eye - 0.75 * (after + square) + 0.25 * both
+
+    def three_steps(step, carry):
+        square, inverse = carry
+        second, factor = two_steps(square)
+        once, twice = times(square, factor), times(second, factor)
+        squared = times(factor, factor)
+        product = 1.5 * factor - 0.5 * times(once, squared)
+        moved = 1.5 * once - 0.5 * times(twice, squared)
+        return times(moved, product), times(product, inverse)
+
+    square, inverse = lax.fori_loop(0, (NS_ITERS - 2) // 3, three_steps, (amat / trace, eye))
+    scale = 1.0 / jnp.sqrt(trace)
+    early = times(inverse, proj)
+    _, factor = two_steps(square)
+    inverse = times(factor, inverse)
+    wbar = times(inverse, times(factor, early)) / trace
+    wtot = (members - 1.0) ** 0.5 * (inverse * scale) + wbar
     mean = jnp.sum(wtot, axis=0, keepdims=True) * (1.0 / members)
     mix = jnp.transpose(blocks(wtot - mean + 1.0 / members))
     mix_high, mix_low = split(mix)
     mix_both = jnp.concatenate([mix_high, mix_low], axis=0)
 
-    for chunk in range(2):
-        group_done(group_recv, 2 + chunk, slab_in.at[chunk], others * slab)
-        for field in range(2):
+    for chunk, fields in enumerate(BACK):
+        for field in fields:
+            for coming, arriving in enumerate(OUTWARD):
+                if field == arriving[0]:
+                    slabs_done(group_recv, 2 + coming, slab_in, arriving)
             lines = [
                 [
-                    slab_in[chunk, pl.ds(field * 8 + at * 2 + row, members, stride=slab), :]
+                    slab_in[field, pl.ds(at * 2 + row, members, stride=slab), :]
                     for at in range(lane_tiles)
                 ]
                 for row in range(2)
@@ -542,27 +569,25 @@
             for row in range(2):
                 for at in range(lane_tiles):
                     patch = row * 2 + at // 2
-                    mix_out[
-                        chunk, pl.ds(field * 8 + at * 2 + row, members, stride=slab), :
-                    ] = mixed[
+                    mix_out[field, pl.ds(at * 2 + row, members, stride=slab), :] = mixed[
                         patch * members : (patch + 1) * members,
                         (at % 2) * LANES : (at % 2 + 1) * LANES,
                     ]
-        back_in[chunk, own_slab, :] = mix_out[chunk, own_slab, :]
+            back_in[field, own_slab, :] = mix_out[field, own_slab, :]
         to_group(
             4 + chunk,
-            lambda peer: slab_of(mix_out, chunk, peer),
-            back_in.at[chunk, own_slab],
+            lambda peer: slab_of(mix_out, fields, peer),
+            slab_of(back_in, fields, me),
         )
-    for chunk in range(2):
-        group_done(group_recv, 4 + chunk, back_in.at[chunk], others * slab)
-        for field in range(2):
+    for chunk, fields in enumerate(BACK):
+        slabs_done(group_recv, 4 + chunk, back_in, fields)
+        for field in fields:
             for at in range(lane_tiles):
                 for row in range(2):
-                    rows_out[2 * chunk + field, at, pl.ds(row, members, stride=2), :] = back_in[
-                        chunk, pl.ds(field * 8 + at * 2 + row, members, stride=slab), :
+                    rows_out[field, at, pl.ds(row, members, stride=2), :] = back_in[
+                        field, pl.ds(at * 2 + row, members, stride=slab), :
                     ]
-        for field in range(2 * chunk, 2 * chunk + 2):
+        for field in fields:
             for at in range(lane_tiles):
                 out_ref[0, field, :, at * LANES : (at + 1) * LANES] = rows_out[field, at]
 
@@ -570,9 +595,10 @@
         copy.wait_send()
     group_done(group_send, 0, lists, others)
     group_done(group_send, 1, pick_out, others)
-    for chunk in range(2):
-        group_done(group_send, 2 + chunk, slab_out.at[chunk], others * slab)
-        group_done(group_send, 4 + chunk, mix_out.at[chunk], others * slab)
+    for chunk, fields in enumerate(OUTWARD):
+        slabs_done(group_send, 2 + chunk, slab_out, fields)
+    for chunk, fields in enumerate(BACK):
+        slabs_done(group_send, 4 + chunk, mix_out, fields)
 
 
 def body(
@@ -593,7 +619,7 @@
     lane_tiles = width // LANES
     own_table = obs_cell.shape[0] // LANES
     table_rows = own_table + 2 * TABLE_PAD
-    slab_rows = members * 4 * lane_tiles
+    slab_rows = members * 2 * lane_tiles
     strip = 2 * HALO + 2 * GUARD
     deep = ext_rows + 2 * GUARD
     as_lines = lambda array: array.reshape(own_table, LANES)
@@ -627,16 +653,16 @@
             pltpu.VMEM((table_rows, LANES), F32),
             pltpu.VMEM((members, 2, LANES), F32),
             pltpu.VMEM((members, 2, LANES), F32),
-            pltpu.VMEM((2, slab_rows, LANES), F32),
-            pltpu.VMEM((2, slab_rows, LANES), F32),
-            pltpu.VMEM((2, slab_rows, LANES), F32),
-            pltpu.VMEM((2, slab_rows, LANES), F32),
+            pltpu.VMEM((4, slab_rows, LANES), F32),
+            pltpu.VMEM((4, slab_rows, LANES), F32),
+            pltpu.VMEM((4, slab_rows, LANES), F32),
+            pltpu.VMEM((4, slab_rows, LANES), F32),
             pltpu.VMEM((4, lane_tiles, grid_rows, LANES), F32),
             pltpu.SemaphoreType.DMA((9,)),
             pltpu.SemaphoreType.DMA((2, 7)),
             pltpu.SemaphoreType.DMA((2, 7)),
-            pltpu.SemaphoreType.DMA((6,)),
-            pltpu.SemaphoreType.DMA((6,)),
+            pltpu.SemaphoreType.DMA((4 + len(BACK),)),
+            pltpu.SemaphoreType.DMA((4 + len(BACK),)),
         ],
         compiler_params=pltpu.CompilerParams(
             collective_id=0, has_side_effects=True, vmem_limit_bytes=32 * 1024 * 1024

time: 43 us -> 42.9 us (level)
  no operation moved by 1% of the time
where the time goes in v3:
time: 42.9 us
  Pallas kernels  42 us (98%)
  local copies, waits for them, and re-layouts  0.8 us (2%)
    pallas_call x1, Pallas kernels, body(): pl.pallas_call(functools.partial(kernel, members, tiles, grid_rows), out_...  42 us

profile of v3, /device:TPU:5, one launch (start us, length us, event | category | flops | bytes accessed | tf_op | source)
XLA Modules:
  0.0 42.9 jit_solution(6856779327812717216)
XLA Ops:
  0.0 42.0 %shard_map.91 = f32[1,4,64,512]{3,2,1,0:T(8,128)S(1)} custom-call(f32[1,4,64,512]{3,2,1,0:T(8,128)} %state_ref.1, f32[64,512]{1,0:T(8,128)} %depth_ref.1, s32[64,512]{1,0:T(8,128)} %wet_ref.1, s32[32,128]{1,0:T(8,128)} %bitcast.4, f32[32,128]{1,0:T(8,128)} %bitcast.5, f32[32,128]{1,0:T(8,128)} %bitcast.6, f32[32,128]{1,0:T(8,128)} %bitcast.7, ...), custom_call_target="tpu_custom_call" | custom-call | tf_op jit(solution)/shard_map/pallas_call | solution.py:628
  42.1 0.8 %copy.11 = f32[1,4,64,512]{3,2,1,0:T(8,128)} copy(f32[1,4,64,512]{3,2,1,0:T(8,128)S(1)} %shard_map.91) | data formatting | bytes 1048576

commit v4 on v3

--- a/solution.py
+++ b/solution.py
@@ -58,11 +58,17 @@
     left_high, left_middle, left_low = split3(left)
     right_high, right_middle, right_low = split3(right)
     rows = left.shape[0]
-    first = dot(jnp.concatenate([left_high, left_middle, left_low], axis=0), right_high)
-    second = dot(jnp.concatenate([left_high, left_middle], axis=0), right_middle)
-    third = dot(left_high, right_low)
-    small = first[2 * rows :] + second[rows:] + third
-    return (small + (first[rows : 2 * rows] + second[:rows])) + first[:rows]
+    straight = jnp.concatenate([left_high, left_middle], axis=1)
+    crossed = jnp.concatenate([left_middle, left_high], axis=1)
+    large = dot(
+        jnp.concatenate([straight, crossed], axis=0),
+        jnp.concatenate([right_high, right_middle], axis=0),
+    )
+    small = dot(
+        jnp.concatenate([left_low, left_high], axis=1),
+        jnp.concatenate([right_high, right_low], axis=0),
+    )
+    return (small + large[rows:]) + large[:rows]
 
 
 def exact_dot(left, ones):
@@ -123,7 +129,6 @@
     slab_in,
     mix_out,
     back_in,
-    rows_out,
     local_sem,
     halo_send,
     halo_recv,
@@ -279,7 +284,7 @@
                 spill = (flux[at, after, :] - flux[at, before, :]) + cross[at, rows, :]
                 fields[0, at, rows, :] = wet * (level - DIVERGE * spill + FORCING * energy)
                 fields[3, at, rows, :] = wet * (
-                    energy - UPWIND * (energy - fields[3, at, before, :]) - DAMPING * energy
+                    (1.0 - UPWIND - DAMPING) * energy + UPWIND * fields[3, at, before, :]
                 )
 
     def inner_step(step, carry):
@@ -344,12 +349,9 @@
 
     def build(field, first, last):
         for at in range(lane_tiles):
-            for row in range(2):
-                slab_out[
-                    field, pl.ds(first * slab + at * 2 + row, last - first, stride=slab), :
-                ] = work[
-                    field, at, pl.ds(own_start + 2 * first + row, last - first, stride=2), :
-                ]
+            slab_out[
+                field, pl.ds(first * slab + at, 2 * (last - first), stride=lane_tiles), :
+            ] = work[field, at, own_start + 2 * first : own_start + 2 * last, :]
 
     def slab_of(ref, fields, owner):
         return ref.at[
@@ -485,6 +487,7 @@
     same = line == column
     diagonal = iota((members, size), 0) == iota((members, size), 1) % members
     eye = jnp.where(diagonal, 1.0, 0.0)
+    ones = jnp.where(same, 1.0, 0.0).astype(BF16)
     patch_ones = (iota((2 * LANES, size), 0) // 64 == iota((2 * LANES, size), 1) // members)
     patch_ones = jnp.where(patch_ones, 1.0, 0.0).astype(BF16)
 
@@ -501,14 +504,17 @@
     by_patch = jnp.where(
         patch_of_line == patch_of_slot, jnp.concatenate([spread] * 4, axis=0), 0.0
     )
-    gram = lax.dot_general(
-        weighted, by_patch, (((1,), (1,)), ((), ())), precision=HIGH, preferred_element_type=F32
-    )
-    sums = exact_dot(
-        jnp.concatenate([weighted * (value - mean_eq), weighted * spread], axis=0), patch_ones
-    )
-    proj = sums[:members]
-    trace = jnp.sum(sums[members:], axis=0, keepdims=True) + (members - 1.0) * members
+    innovation = jnp.broadcast_to(precision * (value - mean_eq), weighted.shape)
+    sums = lax.dot_general(
+        jnp.concatenate([weighted, innovation], axis=0),
+        by_patch,
+        (((1,), (1,)), ((), ())),
+        precision=HIGH,
+        preferred_element_type=F32,
+    )
+    gram, proj = sums[:members], sums[members:]
+    squares = exact_dot(weighted * spread, patch_ones)
+    trace = jnp.sum(squares, axis=0, keepdims=True) + (members - 1.0) * members
 
     amat = gram + (members - 1.0) * eye
 
@@ -532,14 +538,16 @@
         return times(moved, product), times(product, inverse)
 
     square, inverse = lax.fori_loop(0, (NS_ITERS - 2) // 3, three_steps, (amat / trace, eye))
-    scale = 1.0 / jnp.sqrt(trace)
-    early = times(inverse, proj)
+    scale = (members - 1.0) ** 0.5 / jnp.sqrt(trace)
+    early = times(proj, inverse)
+    total = exact_dot(inverse, ones)
     _, factor = two_steps(square)
+    early = times(early, factor)
     inverse = times(factor, inverse)
-    wbar = times(inverse, times(factor, early)) / trace
-    wtot = (members - 1.0) ** 0.5 * (inverse * scale) + wbar
-    mean = jnp.sum(wtot, axis=0, keepdims=True) * (1.0 / members)
-    mix = jnp.transpose(blocks(wtot - mean + 1.0 / members))
+    total = times(factor, total)
+    wbar = times(early, inverse) - times(early, total) * (1.0 / members)
+    mix = scale * (inverse - total * (1.0 / members)) + wbar / trace + 1.0 / members
+    mix = blocks(mix)
     mix_high, mix_low = split(mix)
     mix_both = jnp.concatenate([mix_high, mix_low], axis=0)
 
@@ -550,7 +558,7 @@
                     slabs_done(group_recv, 2 + coming, slab_in, arriving)
             lines = [
                 [
-                    slab_in[field, pl.ds(at * 2 + row, members, stride=slab), :]
+                    slab_in[field, pl.ds(row * lane_tiles + at, members, stride=slab), :]
                     for at in range(lane_tiles)
                 ]
                 for row in range(2)
@@ -569,7 +577,9 @@
             for row in range(2):
                 for at in range(lane_tiles):
                     patch = row * 2 + at // 2
-                    mix_out[field, pl.ds(at * 2 + row, members, stride=slab), :] = mixed[
+                    mix_out[
+                        field, pl.ds(row * lane_tiles + at, members, stride=slab), :
+                    ] = mixed[
                         patch * members : (patch + 1) * members,
                         (at % 2) * LANES : (at % 2 + 1) * LANES,
                     ]
@@ -583,13 +593,9 @@
         slabs_done(group_recv, 4 + chunk, back_in, fields)
         for field in fields:
             for at in range(lane_tiles):
-                for row in range(2):
-                    rows_out[field, at, pl.ds(row, members, stride=2), :] = back_in[
-                        field, pl.ds(at * 2 + row, members, stride=slab), :
-                    ]
-        for field in fields:
-            for at in range(lane_tiles):
-                out_ref[0, field, :, at * LANES : (at + 1) * LANES] = rows_out[field, at]
+                out_ref[0, field, :, at * LANES : (at + 1) * LANES] = back_in[
+                    field, pl.ds(at, grid_rows, stride=lane_tiles), :
+                ]
 
     for copy in halos:
         copy.wait_send()
@@ -657,7 +663,6 @@
             pltpu.VMEM((4, slab_rows, LANES), F32),
             pltpu.VMEM((4, slab_rows, LANES), F32),
             pltpu.VMEM((4, slab_rows, LANES), F32),
-            pltpu.VMEM((4, lane_tiles, grid_rows, LANES), F32),
             pltpu.SemaphoreType.DMA((9,)),
             pltpu.SemaphoreType.DMA((2, 7)),
             pltpu.SemaphoreType.DMA((2, 7)),

time: 42.9 us -> 42.5 us (level)
  no operation moved by 1% of the time
where the time goes in v4:
time: 42.5 us; the launch traced here: 42.4 us
  Pallas kernels  41.6 us (98%)
  local copies, waits for them, and re-layouts  0.8 us (2%)
    pallas_call x1, Pallas kernels, body(): pl.pallas_call(functools.partial(kernel, members, tiles, grid_rows), out_...  41.6 us

profile of v4, /device:TPU:5, one launch (start us, length us, event | category | flops | bytes accessed | tf_op | source)
XLA Modules:
  0.0 42.4 jit_solution(6964288950589504282)
XLA Ops:
  0.0 41.6 %shard_map.91 = f32[1,4,64,512]{3,2,1,0:T(8,128)S(1)} custom-call(f32[1,4,64,512]{3,2,1,0:T(8,128)} %state_ref.1, f32[64,512]{1,0:T(8,128)} %depth_ref.1, s32[64,512]{1,0:T(8,128)} %wet_ref.1, s32[32,128]{1,0:T(8,128)} %bitcast.4, f32[32,128]{1,0:T(8,128)} %bitcast.5, f32[32,128]{1,0:T(8,128)} %bitcast.6, f32[32,128]{1,0:T(8,128)} %bitcast.7, ...), custom_call_target="tpu_custom_call" | custom-call | tf_op jit(solution)/shard_map/pallas_call | solution.py:634
  41.6 0.8 %copy.11 = f32[1,4,64,512]{3,2,1,0:T(8,128)} copy(f32[1,4,64,512]{3,2,1,0:T(8,128)S(1)} %shard_map.91) | data formatting | bytes 1048576

commit v5 on v4

--- a/solution.py
+++ b/solution.py
@@ -252,27 +252,32 @@
             for at in range(lane_tiles)
         ]
 
-    def advance(fields, flux, cross, first, last, shift):
+    def advance(fields, flux, cross, first, last, shift, margin=0):
         for start in range(first, last, 8):
             rows = slice(start, start + 8)
             fixed = slice(start + shift, start + shift + 8)
             after = slice(start + 1, start + 9)
             before = slice(start - 1, start + 7)
-            slope_y = across([fields[0, at, rows, :] for at in range(lane_tiles)])
+            whole = first + margin <= start < last - margin
+            if whole:
+                slope_y = across([fields[0, at, rows, :] for at in range(lane_tiles)])
             flow = []
             for at in range(lane_tiles):
                 wet = wwork[at, fixed, :]
                 height = hwork[at, fixed, :]
                 slope_x = fields[0, at, after, :] - fields[0, at, before, :]
                 new_x = wet * (FRICTION * fields[1, at, rows, :] - PRESSURE * slope_x)
+                flux[at, rows, :] = height * new_x
+                if not whole:
+                    continue
                 new_y = wet * (FRICTION * fields[2, at, rows, :] - PRESSURE * slope_y[at])
                 fields[1, at, rows, :] = new_x
                 fields[2, at, rows, :] = new_y
-                flux[at, rows, :] = height * new_x
                 flow.append(height * new_y)
-            for at, part in enumerate(across(flow)):
-                cross[at, rows, :] = part
-        for start in range(last - 8, first - 8, -8):
+            if whole:
+                for at, part in enumerate(across(flow)):
+                    cross[at, rows, :] = part
+        for start in range(last - margin - 8, first + margin - 8, -8):
             rows = slice(start, start + 8)
             fixed = slice(start + shift, start + shift + 8)
             after = slice(start + 1, start + 9)
@@ -316,8 +321,11 @@
                 device_id={"tile": target},
                 device_id_type=MESH,
             )
-            copy.start()
             halos.append(copy)
+
+    for i in range(7):
+        for way in range(2):
+            halos[way * 7 + i].start()
 
     def send(which, peer, source, destination):
         pltpu.make_async_remote_copy(
@@ -394,7 +402,7 @@
             [(edge.at[1], slice(GUARD + at_row, GUARD + at_row + 8))],
         )
 
-    def edge_step(step, carry):
+    def edge_step(margin):
         for side in range(2):
             advance(
                 edge.at[side],
@@ -403,16 +411,24 @@
                 GUARD,
                 GUARD + strip,
                 edge_starts[side],
+                margin,
             )
+
+    def outer_step(step, carry):
+        edge_step(0)
         return carry
 
-    lax.fori_loop(0, STEPS, edge_step, 0)
-    for side in range(2):
-        for start in (GUARD + 8, GUARD + 16):
-            for field in range(4):
+    lax.fori_loop(0, STEPS - 1, outer_step, 0)
+    edge_step(8)
+
+    def from_edges(field):
+        for side in range(2):
+            for start in (GUARD + 8, GUARD + 16):
                 for at in range(lane_tiles):
                     put = start + edge_starts[side]
                     work[field, at, put : put + 8, :] = edge[side, field, at, start : start + 8, :]
+
+    from_edges(0)
 
     first_line = TABLE_PAD - OBS_HALO // 2
     last_line = TABLE_PAD + own_table + OBS_HALO // 2
@@ -447,6 +463,8 @@
     pick_in[me] = pick_out[me]
     to_group(1, lambda peer: pick_out.at[peer], pick_in.at[me])
 
+    for field in range(1, 4):
+        from_edges(field)
     for field in range(4):
         build(field, 0, edge_owners)
         build(field, members - edge_owners, members)

time: 42.5 us -> 42.8 us (level)
  no operation moved by 1% of the time
where the time goes in v5:
time: 42.8 us; the launch traced here: 42.7 us
  Pallas kernels  41.9 us (98%)
  local copies, waits for them, and re-layouts  0.8 us (2%)
    pallas_call x1, Pallas kernels, body(): pl.pallas_call(functools.partial(kernel, members, tiles, grid_rows), out_...  41.9 us

profile of v5, /device:TPU:5, one launch (start us, length us, event | category | flops | bytes accessed | tf_op | source)
XLA Modules:
  0.0 42.7 jit_solution(11405018892847123423)
XLA Ops:
  0.0 41.9 %shard_map.91 = f32[1,4,64,512]{3,2,1,0:T(8,128)S(1)} custom-call(f32[1,4,64,512]{3,2,1,0:T(8,128)} %state_ref.1, f32[64,512]{1,0:T(8,128)} %depth_ref.1, s32[64,512]{1,0:T(8,128)} %wet_ref.1, s32[32,128]{1,0:T(8,128)} %bitcast.4, f32[32,128]{1,0:T(8,128)} %bitcast.5, f32[32,128]{1,0:T(8,128)} %bitcast.6, f32[32,128]{1,0:T(8,128)} %bitcast.7, ...), custom_call_target="tpu_custom_call" | custom-call | tf_op jit(solution)/shard_map/pallas_call | solution.py:652
  41.9 0.8 %copy.11 = f32[1,4,64,512]{3,2,1,0:T(8,128)} copy(f32[1,4,64,512]{3,2,1,0:T(8,128)S(1)} %shard_map.91) | data formatting | bytes 1048576

commit v6 on v5

--- a/solution.py
+++ b/solution.py
@@ -460,8 +460,8 @@
         )
         for i in range(4):
             pick_out[start + i] = found[2 * i : 2 * i + 2, :]
+    to_group(1, lambda peer: pick_out.at[peer], pick_in.at[me])
     pick_in[me] = pick_out[me]
-    to_group(1, lambda peer: pick_out.at[peer], pick_in.at[me])
 
     for field in range(1, 4):
         from_edges(field)
@@ -601,12 +601,13 @@
                         patch * members : (patch + 1) * members,
                         (at % 2) * LANES : (at % 2 + 1) * LANES,
                     ]
-            back_in[field, own_slab, :] = mix_out[field, own_slab, :]
         to_group(
             4 + chunk,
             lambda peer: slab_of(mix_out, fields, peer),
             slab_of(back_in, fields, me),
         )
+        for field in fields:
+            back_in[field, own_slab, :] = mix_out[field, own_slab, :]
     for chunk, fields in enumerate(BACK):
         slabs_done(group_recv, 4 + chunk, back_in, fields)
         for field in fields:

time: 42.8 us -> 42.8 us (level)
  no operation moved by 1% of the time
where the time goes in v6:
time: 42.8 us; the launch traced here: 42.7 us
  Pallas kernels  41.9 us (98%)
  local copies, waits for them, and re-layouts  0.8 us (2%)
    pallas_call x1, Pallas kernels, body(): pl.pallas_call(functools.partial(kernel, members, tiles, grid_rows), out_...  41.9 us

profile of v6, /device:TPU:5, one launch (start us, length us, event | category | flops | bytes accessed | tf_op | source)
XLA Modules:
  0.0 42.7 jit_solution(7207400535843732850)
XLA Ops:
  0.0 41.9 %shard_map.91 = f32[1,4,64,512]{3,2,1,0:T(8,128)S(1)} custom-call(f32[1,4,64,512]{3,2,1,0:T(8,128)} %state_ref.1, f32[64,512]{1,0:T(8,128)} %depth_ref.1, s32[64,512]{1,0:T(8,128)} %wet_ref.1, s32[32,128]{1,0:T(8,128)} %bitcast.4, f32[32,128]{1,0:T(8,128)} %bitcast.5, f32[32,128]{1,0:T(8,128)} %bitcast.6, f32[32,128]{1,0:T(8,128)} %bitcast.7, ...), custom_call_target="tpu_custom_call" | custom-call | tf_op jit(solution)/shard_map/pallas_call | solution.py:653
  41.9 0.8 %copy.11 = f32[1,4,64,512]{3,2,1,0:T(8,128)} copy(f32[1,4,64,512]{3,2,1,0:T(8,128)S(1)} %shard_map.91) | data formatting | bytes 1048576
